TPU v7x, 256 devices: a whole 4x4x8 slice. The times are simulated.
256 devices in a mesh: member: 32 (over x, y, core), space: 8 (over z).
Axes of the slice: x: 4, y: 4, z: 8, core: 2. Of those that a mesh axis runs over, the one named last changes fastest.
Arguments:
- realization_fields: float32 [32, 4, 16, 16384], P('member', None, 'space'), may hold values from -6 to 6
- viscosity: float32 [16, 16384], P('space'), may hold values from 0.01 to 0.08
- cell_index: int32 [8, 65536], P('space'), may hold values from 0 to 1023
- beam_id: int32 [8, 65536], P('space'), may hold values from 0 to 16383
- los_weight: float32 [8, 3, 65536], P('space'), may hold values from -0.625 to 0.625
- observed: float32 [16384], replicated, may hold values from -16 to 16
- obs_variance: float32 [16384], replicated, may hold values from 64 to 256
Outputs:
- analysis: float32 [32, 4, 16, 16384], P('member', None, 'space')
- mixing: float32 [32, 32], replicated
All inputs are finite; a program needn't handle non-finite values.
Results may differ from a plain program's by a relative error of at most 0.00014.
Values sent between devices are 32-bit elements; how exact they have to be, the bound alone decides.
A program may use at most 192 MiB of HBM per device.

v0:
```python
import jax
import jax.numpy as jnp
from jax import lax
from jax.sharding import PartitionSpec as P

CELLS_SECOND_DIM = 256
CELLS_THIRD_DIM = 64
NS_STEPS = 8


COURANT = 0.5
BUOYANCY = 0.2


def with_halo(block, sides, width):
    for axis, dim in sides:
        count = lax.axis_size(axis)
        forward = [(i, i + 1) for i in range(count - 1)]
        forward.append((count - 1, 0))
        backward = [(target, source) for source, target in forward]
        low = lax.ppermute(
            lax.slice_in_dim(block, block.shape[dim] - width, None, axis=dim), axis, forward
        )
        high = lax.ppermute(lax.slice_in_dim(block, 0, width, axis=dim), axis, backward)
        block = jnp.concatenate([low, block, high], axis=dim)
    return block


def advance(extended, viscosity):
    count = extended.shape[2] - 2
    members = extended.shape[0]
    shaped = extended.reshape(members, 4, count + 2, CELLS_SECOND_DIM, CELLS_THIRD_DIM)
    center = shaped[:, :, 1:-1]
    behind = shaped[:, :, :-2]
    ahead = shaped[:, :, 2:]
    lateral = jnp.roll(center, 1, axis=3) + jnp.roll(center, -1, axis=3)
    bordered_field = jnp.pad(center, ((0, 0), (0, 0), (0, 0), (0, 0), (1, 1)))
    vertical = bordered_field[..., 2:] + bordered_field[..., :-2]
    laplace = behind + ahead + lateral + vertical - 6.0 * center
    viscous = viscosity.reshape(count, CELLS_SECOND_DIM, CELLS_THIRD_DIM)
    moved = center - COURANT * (center - behind) + viscous * laplace
    lifted = moved[:, 2] + BUOYANCY * center[:, 3]
    cooled = moved[:, 3] - BUOYANCY * center[:, 2]
    result = jnp.stack([moved[:, 0], moved[:, 1], lifted, cooled], axis=1)
    return result.reshape(members, 4, count, CELLS_SECOND_DIM * CELLS_THIRD_DIM)


def innovation_stats(predicted, observed, obs_variance):
    mean_pred = jnp.mean(predicted, axis=0)
    anomaly = predicted - mean_pred[None]
    scaled = anomaly / obs_variance[None]
    covar = jnp.dot(scaled, anomaly.T, precision=lax.Precision.HIGHEST)
    drive = jnp.dot(scaled, observed - mean_pred, precision=lax.Precision.HIGHEST)
    return (covar, drive)


def ensemble_transform(covar, drive):
    count = covar.shape[0]
    identity = jnp.eye(count, dtype=jnp.float32)
    system = identity + covar / (count - 1.0)
    magnitude = jnp.sqrt(jnp.sum(system * system))
    iterate = system / magnitude
    inverse_root = identity
    for sweep_index in range(NS_STEPS):
        factor = 1.5 * identity - 0.5 * jnp.dot(
            inverse_root, iterate, precision=lax.Precision.HIGHEST
        )
        iterate = jnp.dot(iterate, factor, precision=lax.Precision.HIGHEST)
        inverse_root = jnp.dot(factor, inverse_root, precision=lax.Precision.HIGHEST)
    root_part = inverse_root / jnp.sqrt(magnitude)
    inverse_full = jnp.dot(inverse_root, inverse_root, precision=lax.Precision.HIGHEST) / magnitude
    shift = jnp.dot(inverse_full, drive, precision=lax.Precision.HIGHEST) / (count - 1.0)
    combined = root_part + shift[:, None]
    return combined - jnp.mean(combined, axis=0, keepdims=True) + 1.0 / count


def project(fields_flat, cells, weights, beams, beam_count):
    values = jnp.take(fields_flat[:, :3], cells, axis=2)
    sightline = jnp.sum(values * weights[None], axis=1)
    return jax.ops.segment_sum(sightline.T, beams, num_segments=beam_count).T


def shards(realization_fields, viscosity, cell_index, beam_id, los_weight, observed, obs_variance):
    local_members, fields, rows, plane = realization_fields.shape
    beam_count = observed.shape[0]
    present_guess = realization_fields
    for sweep_index in range(2):
        extended = with_halo(present_guess, (("space", 2),), 1)
        present_guess = advance(extended, viscosity)
    flattened = present_guess.reshape(local_members, fields, rows * plane)
    pointwise = lax.all_to_all(flattened, "member", split_axis=2, concat_axis=0, tiled=True)
    groups = lax.axis_size("member")
    samples = cell_index.shape[1] // groups
    start = lax.axis_index("member") * samples
    local_cells = lax.dynamic_slice_in_dim(cell_index[0], start, samples)
    local_beams = lax.dynamic_slice_in_dim(beam_id[0], start, samples)
    local_weights = lax.dynamic_slice_in_dim(los_weight[0], start, samples, 1)
    incomplete_total = project(pointwise, local_cells, local_weights, local_beams, beam_count)
    predicted = lax.psum(incomplete_total, ("member", "space"))
    covar, drive = innovation_stats(predicted, observed, obs_variance)
    mixing = ensemble_transform(covar, drive)
    analysed = jnp.einsum("ij,ifp->jfp", mixing, pointwise, precision=lax.Precision.HIGHEST)
    output_result = lax.all_to_all(analysed, "member", split_axis=0, concat_axis=2, tiled=True)
    return (output_result.reshape(realization_fields.shape), mixing)


def solution(mesh):
    return jax.shard_map(
        shards,
        mesh=mesh,
        in_specs=(
            P("member", None, "space", None),
            P("space", None),
            P("space", None),
            P("space", None),
            P("space", None, None),
            P(),
            P(),
        ),
        out_specs=(P("member", None, "space", None), P()),
        check_vma=False,
    )
```

profile of v0, /device:TPU:1, one launch (start us, length us, event | category | flops | bytes accessed | tf_op | source)
XLA Modules:
  0.0 685.1 jit_solution(8428418132513639187)
XLA Ops:
  7.2 1.7 fusion.53
  8.9 2.5 collective-permute-start
  11.5 4.0 collective-permute-start.1
  15.5 1.1 mul.119
  16.6 4.8 collective-permute-done
  21.4 2.7 pad_maximum_fusion
  24.2 2.1 reshape.200
  26.3 0.2 fusion.50
  26.6 0.8 fusion.35
  27.4 0.8 fusion.39
  28.2 1.1 stack.25
  29.3 0.3 stack.24
  29.6 0.1 stack.26
  29.8 0.4 fusion.52
  30.3 3.1 collective-permute-start.3
  33.4 0.7 compare_select_fusion
  34.2 3.9 collective-permute-done.2
  38.1 1.7 pad_maximum_fusion.1
  39.8 2.1 reshape.201
  41.9 0.2 fusion.48
  42.2 0.8 fusion.30
  43.1 0.3 stack.28
  43.4 0.2 stack.29
  43.6 0.2 stack.30
  43.8 0.3 pad_maximum_fusion.2
  44.1 23.9 %copy.21 = f32[1,4,32768]{1,0,2:T(1,128)} copy(f32[1,4,32768]{2,1,0:T(4,128)S(1)} %pad_maximum_fusion.2) | data formatting | bytes 1048576 | tf_op jit(solution)/shard_map/stack | solution.py:44
  68.0 0.5 broadcast.121
  68.5 146.5 %reduce = f32[32768,4]{1,0:T(8,128)} reduce(f32[32768,1,4]{2,1,0:T(1,128)} %bitcast.97, f32[]{:T(128)} %broadcast.121), dimensions={1}, to_apply=%bitcast.48.reduce_sub_computation | reduce | bytes 1048580
  215.0 16.0 %reshape.227 = f32[32,1,4096]{2,1,0:T(1,128)} reshape(f32[32768,4]{1,0:T(8,128)} %reduce) | data formatting | bytes 1048576
  231.0 9.2 %all-to-all-start = ((f32[32,1,4096]{2,1,0:T(1,128)}), f32[32,1,4096]{2,1,0:T(1,128)S(1)}, u32[]{:S(2)}, u32[]{:S(2)}) async-start(f32[32,1,4096]{2,1,0:T(1,128)} %reshape.227), calls=%async_computation | async-start | bytes 1048576 | tf_op jit(solution)/shard_map/all_to_all | solution.py:91
  240.2 0.2 all-reduce.4.cloned.1.call-start
  240.5 0.7 constant_dynamic-slice_fusion.2
  241.2 1.4 copy.30
  242.5 9.3 %all-to-all-done = f32[32,1,4096]{2,1,0:T(1,128)S(1)} async-done(((f32[32,1,4096]{2,1,0:T(1,128)}), f32[32,1,4096]{2,1,0:T(1,128)S(1)}, u32[]{:S(2)}, u32[]{:S(2)}) %all-to-all-start) | async-done | bytes 524320 | tf_op jit(solution)/shard_map/all_to_all | solution.py:91
  251.9 1.9 reduce.1
  253.8 29.1 %reshape.228 = f32[32768,1,4]{2,1,0:T(1,128)} reshape(f32[32,4096]{1,0:T(8,128)S(1)} %reduce.1) | data formatting | bytes 1048576
  282.9 10.0 %copy.29 = f32[1,4,32,1024]{3,2,1,0:T(8,128)S(1)} copy(f32[1,4,32,1024]{1,3,2,0:T(8,128)} %bitcast.98) | data formatting | bytes 1048576 | tf_op jit(solution)/shard_map/all_to_all | solution.py:91
  293.0 0.9 copy.23
  293.8 15.3 %gather_fusion = f32[2048,32,3]{1,2,0:T(4,128)} fusion(f32[32,3,1024]{0,1,2:T(4,128)S(1)} %copy.23, s32[2048]{0:T(1024)S(1)} %broadcast_clamp_fusion), kind=kCustom, calls=%fused_computation | custom fusion | bytes 1581056 | tf_op jit(solution)/shard_map/jit(_take)/gather | solution.py:78
  309.2 13.1 %fusion.3 = f32[32,2048]{0,1:T(8,128)S(1)} fusion(f32[2048,32,3]{1,2,0:T(4,128)} %gather_fusion, f32[3,2048]{0,1:T(8,128)} %bitcast.100, pred[2048]{0:T(1024)(128)(4,1)S(1)} %compare_and_fusion), kind=kLoop, calls=%fused_computation.7 | loop fusion | flops 524288 | bytes 1075200 | tf_op jit(solution)/shard_map/reduce_sum | solution.py:79
  322.3 15.4 %scatter_custom_fusion = f32[16384,32]{1,0:T(8,128)} fusion(s32[2048]{0:T(1024)S(1)} %bitcast.106, f32[]{:T(128)} %constant.18.clone.1, f32[32,2048]{0,1:T(8,128)S(1)} %fusion.3), kind=kCustom, calls=%fused_computation.12 | custom fusion | flops 65536 | bytes 3145732 | tf_op jit(solution)/shard_map/scatter-add | solution.py:80
  337.8 273.9 %all-reduce.4.cloned.1.call-done = f32[32,16384]{0,1:T(8,128)} async-done(((f32[32,16384]{0,1:T(8,128)}), f32[32,16384]{0,1:T(8,128)}) %all-reduce.4.cloned.1.call-update) | async-done | bytes 2097168 | tf_op jit(solution)/shard_map/psum | solution.py:99
  611.7 4.6 reduce_sum.37
  616.4 24.1 %multiply_reduce_fusion = (f32[]{:T(128)}, f32[32,32]{1,0:T(8,128)S(1)}) fusion(f32[32,16384]{0,1:T(8,128)} %all-reduce.4.cloned.1.call-done, f32[16384]{0:T(1024)S(1)} %get-tuple-element.21, f32[16384]{0:T(1024)S(1)} %copy-done.4), kind=kOutput, calls=%fused_computation.69 | convolution fusion | flops 202905600 | bytes 2232324 | tf_op jit(solution)/shard_map/dot_general | solution.py:52
  641.6 0.2 fusion.16
  641.9 0.1 fusion.54
  642.0 0.2 fusion.15
  642.3 0.1 fusion.56
  642.5 0.2 fusion.14
  642.8 0.1 fusion.58
  642.9 0.2 fusion.13
  643.2 0.1 fusion.60
  643.4 0.2 fusion.12
  643.7 0.1 fusion.62
  643.9 0.2 fusion.11
  644.2 0.1 fusion.64
  644.7 0.2 convolution_divide_fusion
  644.8 10.4 %fusion.24 = f32[32,1]{0,1:T(1,128)S(1)} fusion(f32[16384,1]{0,1:T(1,128)S(1)} %bitcast.103, f32[32,16384]{0,1:T(8,128)} %all-reduce.4.cloned.1.call-done, f32[16384]{0:T(1024)S(1)} %copy-done.4, f32[16384]{0:T(1024)S(1)} %get-tuple-element.21), kind=kOutput, calls=%fused_computation.33 | convolution fusion | flops 7340032 | bytes 2293888 | tf_op jit(solution)/shard_map/dot_general | solution.py:53
  655.3 0.1 fusion.25
  655.6 0.6 fusion.41
  656.2 0.3 copy.26
  656.6 19.9 %all_to_all.33 = f32[32,4,1024]{2,1,0:T(4,128)S(1)} all-to-all(f32[32,4,1024]{2,1,0:T(4,128)S(1)} %copy.26), channel_id=1, replica_groups=mesh['member'=32,'space'=8] {'member'}, dimensions={0} | all-to-all | bytes 1048576 | tf_op jit(solution)/shard_map/all_to_all | solution.py:103
  676.5 0.3 copy.27
  676.8 1.2 reshape.202
  (43 shorter events, 2.2 us)
Async XLA Ops:
  7.2 27.0 %copy-start = (f32[1,3,65536]{2,0,1:T(1,128)S(1)}, f32[1,3,65536]{2,0,1:T(1,128)}, u32[]{:S(2)}) copy-start(f32[1,3,65536]{2,0,1:T(1,128)} %param.11) | copy-start | bytes 2359300
  8.9 12.5 %collective-permute-start = (f32[1,4,1,16384]{3,2,1,0:T(1,128)S(1)}, f32[1,4,1,16384]{3,2,1,0:T(1,128)S(1)}, u32[]{:S(2)}, u32[]{:S(2)}) collective-permute-start(f32[1,4,1,16384]{3,2,1,0:T(1,128)S(1)} %get-tuple-element.18), channel_id=1, source_target_pairs={{0,1},{1,2},{2,3},{3,4},{4,5},{5,6},{6,7},{7,0},{8,9},{9,10},{10,1... | collective-permute-start | bytes 786440 | tf_op jit(solution)/shard_map/ppermute | solution.py:21
  11.5 10.0 %collective-permute-start.1 = (f32[1,4,1,16384]{3,2,1,0:T(1,128)S(1)}, f32[1,4,1,16384]{3,2,1,0:T(1,128)S(1)}, u32[]{:S(2)}, u32[]{:S(2)}) collective-permute-start(f32[1,4,1,16384]{3,2,1,0:T(1,128)S(1)} %get-tuple-element.19), channel_id=1, source_target_pairs={{1,0},{2,1},{3,2},{4,3},{5,4},{6,5},{7,6},{0,7},{9,8},{10,9},{11,1... | collective-permute-start | bytes 786440 | tf_op jit(solution)/shard_map/ppermute | solution.py:24
  30.2 7.9 %collective-permute-start.2 = (f32[1,4,1,16384]{3,2,1,0:T(1,128)S(1)}, f32[1,4,1,16384]{3,2,1,0:T(1,128)S(1)}, u32[]{:S(2)}, u32[]{:S(2)}) collective-permute-start(f32[1,4,1,16384]{3,2,1,0:T(1,128)S(1)} %get-tuple-element.16), channel_id=1, source_target_pairs={{0,1},{1,2},{2,3},{3,4},{4,5},{5,6},{6,7},{7,0},{8,9},{9,10},{10,1... | collective-permute-start | bytes 786440 | tf_op jit(solution)/shard_map/ppermute | solution.py:21
  30.3 7.8 %collective-permute-start.3 = (f32[1,4,1,16384]{3,2,1,0:T(1,128)S(1)}, f32[1,4,1,16384]{3,2,1,0:T(1,128)S(1)}, u32[]{:S(2)}, u32[]{:S(2)}) collective-permute-start(f32[1,4,1,16384]{3,2,1,0:T(1,128)S(1)} %get-tuple-element.17), channel_id=1, source_target_pairs={{1,0},{2,1},{3,2},{4,3},{5,4},{6,5},{7,6},{0,7},{9,8},{10,9},{11,1... | collective-permute-start | bytes 786440 | tf_op jit(solution)/shard_map/ppermute | solution.py:24
  231.0 20.9 %all-to-all-start = ((f32[32,1,4096]{2,1,0:T(1,128)}), f32[32,1,4096]{2,1,0:T(1,128)S(1)}, u32[]{:S(2)}, u32[]{:S(2)}) async-start(f32[32,1,4096]{2,1,0:T(1,128)} %reshape.227), calls=%async_computation | async-start | bytes 1048576 | tf_op jit(solution)/shard_map/all_to_all | solution.py:91
  240.2 371.5 %all-reduce.4.cloned.1.call-start = ((), (), s32[]{:S(2)}) async-start(), calls=%async_computation.2 | async-start | bytes 16777216 | tf_op jit(solution)/shard_map/psum | solution.py:99
  337.7 278.6 %copy-start.3 = (f32[16384]{0:T(1024)S(1)}, f32[16384]{0:T(1024)}, u32[]{:S(2)}) copy-start(f32[16384]{0:T(1024)} %param.12) | copy-start | bytes 196612
  337.7 278.6 %copy-start.4 = (f32[16384]{0:T(1024)S(1)}, f32[16384]{0:T(1024)}, u32[]{:S(2)}) copy-start(f32[16384]{0:T(1024)} %param.13) | copy-start | bytes 196612
  644.8 33.2 %copy-start.1 = (f32[1,3,65536]{2,0,1:T(1,128)S(1)}, f32[1,3,65536]{2,0,1:T(1,128)}, u32[]{:S(2)}) copy-start(f32[1,3,65536]{2,0,1:T(1,128)} %param.11) | copy-start | bytes 2359300
  655.6 22.4 %copy-start.2 = (f32[32,32]{1,0:T(8,128)}, f32[32,32]{1,0:T(8,128)S(1)}, u32[]{:S(2)}) copy-start(f32[32,32]{1,0:T(8,128)S(1)} %subtract_add_fusion) | copy-start | bytes 12292
Sparse Core Ops, SparseCore 0:
  337.9 273.7 all-reduce.3
where the time goes:
time: 692 us; the launch traced here: 685 us
  waiting for transfers between devices  292 us (42%)
  other arithmetic  190 us (27%)
  local copies, waits for them, and re-layouts  110 us (16%)
  matrix products  38.8 us (6%)
  blocking collectives  19.9 us (3%)
  starting transfers between devices  19.2 us (3%)
  between operations  15.5 us (2%)
    psum x1, waiting for transfers between devices, shards(): predicted = lax.psum(incomplete_total, ('member', 'space'))  274 us
    unnamed x1, other arithmetic  147 us
    unnamed x15, local copies, waits for them, and re-layouts  45.7 us
    another operation x8, local copies, waits for them, and re-layouts, advance(): result = jnp.stack([moved[:, 0], moved[:, 1], lifted, cooled], axis=1)  26 us
    dot_general x1, matrix products, innovation_stats(): covar = jnp.dot(scaled, anomaly.T, precision=lax.Precision.HIGHEST)  24.1 us
    all_to_all x1, blocking collectives, shards(): lax.all_to_all(analysed, 'member', split_axis=0, concat_axis=2, tiled=True)  19.9 us
    scatter-add x1, other arithmetic, project(): return jax.ops.segment_sum(sightline.T, beams, num_segments=beam_count).T  15.4 us
    gather x1, local copies, waits for them, and re-layouts, project(): values = jnp.take(fields_flat[:, :3], cells, axis=2)  15.3 us
  transfers between devices with their start and end apart: 6, of which 4 were waited for; matrix products, arithmetic and copies ran while one was open for 1% of the time, Pallas kernels for 0%

commit v1 on v0

v1 whole, which is shorter than its diff:
```python
import functools

import jax
import jax.numpy as jnp
from jax import lax
from jax.experimental import pallas as pl
from jax.experimental.pallas import tpu as pltpu
from jax.sharding import PartitionSpec as P

NS_STEPS = 8
COURANT = 0.5
BUOYANCY = 0.2
FIELDS = 4
LANES = 128
HALF = 64
BEAM_ROWS = 64
BEAM_COLS = 256
PARTS = 3
ORDER = (2, 3, 0, 1)
MESH = pl.DeviceIdType.MESH
F32 = jnp.float32
BF16 = jnp.bfloat16
HIGHEST = lax.Precision.HIGHEST


def bf16_iota(shape, dim):
    return lax.broadcasted_iota(jnp.int32, shape, dim).astype(F32).astype(BF16)


def stencil(center, behind, ahead, viscous):
    lane = lax.broadcasted_iota(jnp.int32, center.shape, 1)
    depth = lane & (HALF - 1)
    rows = center.shape[0]
    swapped = pltpu.roll(center, HALF, 1)
    lateral = swapped + jnp.where(
        lane < HALF, pltpu.roll(swapped, 1, 0), pltpu.roll(swapped, rows - 1, 0)
    )
    above = jnp.where(depth == HALF - 1, 0.0, pltpu.roll(center, LANES - 1, 1))
    below = jnp.where(depth == 0, 0.0, pltpu.roll(center, 1, 1))
    laplace = behind + ahead + lateral + (above + below) - 6.0 * center
    return center - COURANT * (center - behind) + viscous * laplace


def kernel(
    members, spaces,
    fields_ref, visc_ref, cell_ref, beam_ref, weight_ref, observed_ref, variance_ref,
    out_ref, mixing_ref,
    planes, visc, halo_low, halo_high, forecast, pointwise, sight, scatter,
    beam_send, beam_recv, gathered, stats_send, stats_recv, mixed, returned,
    halo_send_sem, halo_recv_sem, there_send_sem, there_recv_sem, beam_send_sem, beam_recv_sem,
    gather_send_sem, gather_recv_sem, stats_send_sem, stats_recv_sem, back_send_sem, back_recv_sem,
):
    me = lax.axis_index("member")
    here = lax.axis_index("space")
    nxt = lax.rem(here + 1, spaces)
    prv = lax.rem(here + spaces - 1, spaces)

    barrier = pltpu.get_barrier_semaphore()

    def greet_space(d, carry):
        pl.semaphore_signal(
            barrier, inc=1, device_id=(me, lax.rem(here + d, spaces)), device_id_type=MESH
        )
        return carry

    def greet_member(d, carry):
        pl.semaphore_signal(
            barrier, inc=1, device_id=(lax.rem(me + d, members), here), device_id_type=MESH
        )
        return carry

    lax.fori_loop(1, spaces, greet_space, 0)
    lax.fori_loop(1, members, greet_member, 0)
    pl.semaphore_wait(barrier, members + spaces - 2)

    def halo_copies(step, f):
        base = (step * FIELDS + f) * 2
        down = pltpu.make_async_remote_copy(
            src_ref=planes.at[step, 0, f], dst_ref=halo_high.at[step, f],
            send_sem=halo_send_sem.at[base], recv_sem=halo_recv_sem.at[base],
            device_id=(me, prv), device_id_type=MESH,
        )
        up = pltpu.make_async_remote_copy(
            src_ref=planes.at[step, 1, f], dst_ref=halo_low.at[step, f],
            send_sem=halo_send_sem.at[base + 1], recv_sem=halo_recv_sem.at[base + 1],
            device_id=(me, nxt), device_id_type=MESH,
        )
        return down, up

    def start_halo(step, f):
        for copy in halo_copies(step, f):
            copy.start()

    def finish_halo(step, f):
        for copy in halo_copies(step, f):
            copy.wait()

    for f in ORDER:
        for r in range(2):
            planes[0, r, f] = fields_ref[f, pl.ds(r, LANES, stride=2), :]
        start_halo(0, f)
    for r in range(2):
        visc[r] = visc_ref[pl.ds(r, LANES, stride=2), :]

    def advance(step, group):
        for f in group:
            finish_halo(step, f)
        for r in range(2):
            moved = []
            for f in group:
                center = planes[step, r, f]
                behind = halo_low[step, f] if r == 0 else planes[step, 0, f]
                ahead = planes[step, 1, f] if r == 0 else halo_high[step, f]
                moved.append(stencil(center, behind, ahead, visc[r]))
            if len(group) == 2:
                moved[0] = moved[0] + BUOYANCY * planes[step, r, group[1]]
                moved[1] = moved[1] - BUOYANCY * planes[step, r, group[0]]
            for f, value in zip(group, moved):
                if step == 0:
                    planes[1, r, f] = value
                else:
                    blocks = members // 2
                    forecast[pl.ds(r * blocks, blocks), f] = value.reshape(blocks, 8, LANES)

    groups = ((2, 3), (0,), (1,))
    for group in groups:
        advance(0, group)
        for f in group:
            start_halo(1, f)
    for group in groups:
        advance(1, group)

    def there(p):
        return pltpu.make_async_remote_copy(
            src_ref=forecast.at[p], dst_ref=pointwise.at[me],
            send_sem=there_send_sem.at[p], recv_sem=there_recv_sem.at[me],
            device_id=(p, here), device_id_type=MESH,
        )

    def there_from(i):
        return pltpu.make_async_remote_copy(
            src_ref=forecast.at[i], dst_ref=pointwise.at[i],
            send_sem=there_send_sem.at[i], recv_sem=there_recv_sem.at[i],
            device_id=(i, here), device_id_type=MESH,
        )

    def others(count, mine, act):
        def one(d, carry):
            act(lax.rem(mine + d, count))
            return carry

        lax.fori_loop(1, count, one, 0)

    others(members, me, lambda p: there(p).start())
    pointwise[me] = forecast[me]

    def gather_block(p):
        for g in range(2):
            rows = pl.ds(pl.multiple_of(16 * p + 8 * g, 8), 8)
            cells = cell_ref[rows, :]
            low, high = cells & (LANES - 1), cells >> 7
            total = None
            for c in range(3):
                table = forecast[p, c]
                value = None
                for t in range(8):
                    row = jnp.broadcast_to(table[t : t + 1], (8, LANES))
                    found = jnp.take_along_axis(row, low, axis=1, mode="promise_in_bounds")
                    value = found if value is None else jnp.where(high == t, found, value)
                term = weight_ref[c, rows, :] * value
                total = term if total is None else total + term
            sight[rows, :] = total

    def scatter_block(p):
        rows = pl.ds(pl.multiple_of(16 * p, 16), 16)
        rest = sight[rows, :]
        beams = beam_ref[rows, :]
        parts = []
        for _ in range(PARTS):
            part = rest.astype(BF16)
            parts.append(part)
            rest = rest - part.astype(F32)
        beam_row = (beams >> 8).astype(F32).astype(BF16)
        beam_col = (beams & (BEAM_COLS - 1)).astype(F32).astype(BF16)
        col_ids = bf16_iota((BEAM_COLS, LANES), 0)
        row_ids = bf16_iota((BEAM_ROWS, LANES), 0)
        ones, zeros = jnp.ones((BEAM_COLS, LANES), BF16), jnp.zeros((BEAM_COLS, LANES), BF16)
        left, right = [], []
        for g in range(16):
            right.append(jnp.where(col_ids == beam_col[g : g + 1], ones, zeros))
            hit = row_ids == beam_row[g : g + 1]
            left.append(jnp.concatenate([
                jnp.where(hit, jnp.broadcast_to(part[g : g + 1], (BEAM_ROWS, LANES)), zeros[:BEAM_ROWS])
                for part in parts
            ], axis=0))
        scatter[...] += lax.dot_general(
            jnp.concatenate(left, axis=1), jnp.concatenate(right, axis=1),
            (((1,), (1,)), ((), ())), preferred_element_type=F32,
        )

    scatter[...] = jnp.zeros_like(scatter)
    gather_block(0)

    def samples(p, carry):
        scatter_block(p - 1)
        gather_block(p)
        return carry

    lax.fori_loop(1, members, samples, 0)
    scatter_block(members - 1)
    total = scatter[0:BEAM_ROWS]
    for i in range(1, PARTS):
        total = total + scatter[BEAM_ROWS * i : BEAM_ROWS * (i + 1)]
    beam_send[...] = total.reshape(beam_send.shape)

    def beam_to(t):
        return pltpu.make_async_remote_copy(
            src_ref=beam_send.at[t], dst_ref=beam_recv.at[here],
            send_sem=beam_send_sem.at[t], recv_sem=beam_recv_sem.at[here],
            device_id=(me, t), device_id_type=MESH,
        )

    def beam_from(t):
        return pltpu.make_async_remote_copy(
            src_ref=beam_send.at[t], dst_ref=beam_recv.at[t],
            send_sem=beam_send_sem.at[t], recv_sem=beam_recv_sem.at[t],
            device_id=(me, t), device_id_type=MESH,
        )

    others(spaces, here, lambda t: beam_to(t).start())
    beam_recv[here] = beam_send[here]
    others(spaces, here, lambda t: beam_from(t).wait_recv())
    predicted = beam_recv[0]
    for t in range(1, spaces):
        predicted = predicted + beam_recv[t]

    def slot(i):
        return gathered.at[pl.ds(pl.multiple_of(16 * i, 16), 16), :]

    def share_to(p):
        return pltpu.make_async_remote_copy(
            src_ref=slot(me), dst_ref=slot(me),
            send_sem=gather_send_sem.at[p], recv_sem=gather_recv_sem.at[me],
            device_id=(p, here), device_id_type=MESH,
        )

    def share_from(i):
        return pltpu.make_async_remote_copy(
            src_ref=slot(i), dst_ref=slot(i),
            send_sem=gather_send_sem.at[i], recv_sem=gather_recv_sem.at[i],
            device_id=(i, here), device_id_type=MESH,
        )

    for half in range(2):
        gathered[pl.ds(pl.multiple_of(16 * me + 8 * half, 8), 8), :] = (
            predicted[:, half * LANES : (half + 1) * LANES]
        )
    others(members, me, lambda p: share_to(p).start())
    others(members, me, lambda i: share_from(i).wait_recv())

    every = jnp.concatenate(
        [
            gathered[pl.ds(8 * half + sub, members, stride=16), :]
            for sub in range(8) for half in range(2)
        ],
        axis=1,
    )
    mine = pl.ds(pl.multiple_of(16 * here, 16), 16)
    seen_rows, var_rows = observed_ref[mine, :], variance_ref[mine, :]
    seen = jnp.concatenate([seen_rows[i : i + 1] for i in range(16)], axis=1)
    variance = jnp.concatenate([var_rows[i : i + 1] for i in range(16)], axis=1)
    mean_pred = jnp.mean(every, axis=0, keepdims=True)
    anomaly = every - mean_pred
    scaled = anomaly / variance
    width = anomaly.shape[1]
    against = jnp.concatenate(
        [anomaly, seen - mean_pred, jnp.zeros((LANES - members - 1, width), F32)], axis=0
    )
    stats_send[...] = lax.dot_general(
        scaled, against, (((1,), (1,)), ((), ())), precision=HIGHEST, preferred_element_type=F32
    )

    def stats_to(t):
        return pltpu.make_async_remote_copy(
            src_ref=stats_send, dst_ref=stats_recv.at[here],
            send_sem=stats_send_sem.at[t], recv_sem=stats_recv_sem.at[here],
            device_id=(me, t), device_id_type=MESH,
        )

    def stats_from(t):
        return pltpu.make_async_remote_copy(
            src_ref=stats_send, dst_ref=stats_recv.at[t],
            send_sem=stats_send_sem.at[t], recv_sem=stats_recv_sem.at[t],
            device_id=(me, t), device_id_type=MESH,
        )

    others(spaces, here, lambda t: stats_to(t).start())
    stats_recv[here] = stats_send[...]
    others(spaces, here, lambda t: stats_from(t).wait_recv())
    stats = stats_recv[0]
    for t in range(1, spaces):
        stats = stats + stats_recv[t]

    def times(a, b):
        return jnp.dot(a, b, precision=HIGHEST, preferred_element_type=F32)

    covar = stats[:, :members]
    row_id = lax.broadcasted_iota(jnp.int32, (members, members), 0)
    col_id = lax.broadcasted_iota(jnp.int32, (members, members), 1)
    identity = jnp.where(row_id == col_id, 1.0, 0.0).astype(F32)
    system = identity + covar / (members - 1.0)
    magnitude = jnp.sqrt(jnp.sum(system * system, axis=(0, 1), keepdims=True))
    iterate = system / magnitude
    inverse_root = identity
    for _ in range(NS_STEPS):
        factor = 1.5 * identity - 0.5 * times(inverse_root, iterate)
        iterate = times(iterate, factor)
        inverse_root = times(factor, inverse_root)
    root_part = inverse_root / jnp.sqrt(magnitude)
    inverse_full = times(inverse_root, inverse_root) / magnitude
    shift = times(inverse_full, stats)[:, members : members + 1] / (members - 1.0)
    combined = root_part + shift
    mixing = combined - jnp.mean(combined, axis=0, keepdims=True) + 1.0 / members
    mixing_ref[...] = mixing

    others(members, me, lambda i: there_from(i).wait_recv())
    count = FIELDS * 8
    block = jnp.concatenate(
        [pointwise.reshape(members * count, LANES)[pl.ds(k, members, stride=count), :] for k in range(count)],
        axis=1,
    )
    analysed = lax.dot_general(
        mixing, block, (((0,), (0,)), ((), ())), precision=HIGHEST, preferred_element_type=F32
    )
    for k in range(count):
        mixed.reshape(members * count, LANES)[pl.ds(k, members, stride=count), :] = (
            analysed[:, k * LANES : (k + 1) * LANES]
        )

    def back(j):
        return pltpu.make_async_remote_copy(
            src_ref=mixed.at[j], dst_ref=returned.at[me],
            send_sem=back_send_sem.at[j], recv_sem=back_recv_sem.at[me],
            device_id=(j, here), device_id_type=MESH,
        )

    def back_from(p):
        return pltpu.make_async_remote_copy(
            src_ref=mixed.at[p], dst_ref=returned.at[p],
            send_sem=back_send_sem.at[p], recv_sem=back_recv_sem.at[p],
            device_id=(p, here), device_id_type=MESH,
        )

    others(members, me, lambda j: back(j).start())
    returned[me] = mixed[me]
    others(members, me, lambda p: there(p).wait_send())
    others(spaces, here, lambda t: beam_to(t).wait_send())
    others(members, me, lambda p: share_to(p).wait_send())
    others(spaces, here, lambda t: stats_to(t).wait_send())
    others(members, me, lambda p: back_from(p).wait_recv())
    for p in range(members):
        r, q = divmod(p, members // 2)
        for f in range(FIELDS):
            out_ref[f, pl.ds(16 * q + r, 8, stride=2), :] = returned[p, f]
    others(members, me, lambda j: back(j).wait_send())


def shards(members, spaces, realization_fields, viscosity, cell_index, beam_id, los_weight, observed, obs_variance):
    _, fields, rows, plane = realization_fields.shape
    lines = plane // LANES
    samples = cell_index.shape[1] // LANES
    beams = observed.shape[0] // LANES
    mixed_rows = realization_fields.reshape(fields, rows, lines, LANES).transpose(0, 2, 1, 3)
    visc_rows = viscosity.reshape(rows, lines, LANES).transpose(1, 0, 2)
    block = (members, FIELDS, 8, LANES)
    share = (BEAM_ROWS // spaces, BEAM_COLS)
    dma = lambda n: pltpu.SemaphoreType.DMA((n,))
    vmem = pl.BlockSpec(memory_space=pltpu.VMEM)
    analysis, mixing = pl.pallas_call(
        functools.partial(kernel, members, spaces),
        out_shape=(
            jax.ShapeDtypeStruct((fields, rows * lines, LANES), F32),
            jax.ShapeDtypeStruct((members, members), F32),
        ),
        in_specs=[vmem] * 7,
        out_specs=(vmem, vmem),
        scratch_shapes=[
            pltpu.VMEM((2, rows, fields, lines, LANES), F32),
            pltpu.VMEM((rows, lines, LANES), F32),
            pltpu.VMEM((2, fields, lines, LANES), F32),
            pltpu.VMEM((2, fields, lines, LANES), F32),
            pltpu.VMEM(block, F32),
            pltpu.VMEM(block, F32),
            pltpu.VMEM((samples, LANES), F32),
            pltpu.VMEM((PARTS * BEAM_ROWS, BEAM_COLS), F32),
            pltpu.VMEM((spaces,) + share, F32),
            pltpu.VMEM((spaces,) + share, F32),
            pltpu.VMEM((members * 2 * share[0], LANES), F32),
            pltpu.VMEM((members, LANES), F32),
            pltpu.VMEM((spaces, members, LANES), F32),
            pltpu.VMEM(block, F32),
            pltpu.VMEM(block, F32),
            dma(4 * fields), dma(4 * fields),
            dma(members), dma(members),
            dma(spaces), dma(spaces),
            dma(members), dma(members),
            dma(spaces), dma(spaces),
            dma(members), dma(members),
        ],
        compiler_params=pltpu.CompilerParams(
            collective_id=0, has_side_effects=True, vmem_limit_bytes=40 << 20
        ),
    )(
        mixed_rows.reshape(fields, lines * rows, LANES),
        visc_rows.reshape(lines * rows, LANES),
        cell_index.reshape(samples, LANES),
        beam_id.reshape(samples, LANES),
        los_weight.reshape(3, samples, LANES),
        observed.reshape(beams, LANES),
        obs_variance.reshape(beams, LANES),
    )
    analysis = analysis.reshape(fields, lines, rows, LANES).transpose(0, 2, 1, 3)
    return analysis.reshape(realization_fields.shape), mixing


def solution(mesh):
    return jax.shard_map(
        functools.partial(shards, mesh.shape["member"], mesh.shape["space"]),
        mesh=mesh,
        in_specs=(
            P("member", None, "space", None),
            P("space", None),
            P("space", None),
            P("space", None),
            P("space", None, None),
            P(),
            P(),
        ),
        out_specs=(P("member", None, "space", None), P()),
        check_vma=False,
    )
```

time: 692 us -> 83.2 us (0.12)
  waiting for transfers between devices: 292 us -> 0 us
  other arithmetic: 190 us -> 0 us
  local copies, waits for them, and re-layouts: 110 us -> 8.05 us
  Pallas kernels: 0 us -> 74.2 us
  matrix products: 38.8 us -> 0 us
  blocking collectives: 19.9 us -> 0 us
  starting transfers between devices: 19.2 us -> 0 us
  between operations: 15.5 us -> 0.66 us
    psum x1 -> x0, waiting for transfers between devices: 274 us -> none  [shards(): predicted = lax.psum(incomplete_total, ('member', 'space'))]
    unnamed x1 -> x0, other arithmetic: 147 us -> none
    pallas_call x0 -> x1, Pallas kernels: none -> 74.2 us  [shards(): pl.pallas_call(functools.partial(kernel, members, spaces), out_shape=(jax...]
    dot_general x28 -> x0, matrix products: 38.8 us -> none  [the longest x1 24.1 us: innovation_stats(): covar = jnp.dot(scaled, anomaly.T, precision=lax.Precision.HIGHEST)]
    unnamed x15 -> x16, local copies, waits for them, and re-layouts: 45.7 us -> 8.05 us
    another operation x8 -> x0, local copies, waits for them, and re-layouts: 26 us -> none  [advance(): result = jnp.stack([moved[:, 0], moved[:, 1], lifted, cooled], axis=1)]
    all_to_all x1 -> x0, blocking collectives: 19.9 us -> none  [shards(): lax.all_to_all(analysed, 'member', split_axis=0, concat_axis=2, tiled=True)]
    reduce_sum x3 -> x0, other arithmetic: 17.9 us -> none  [the longest x1 13.1 us: project(): sightline = jnp.sum(values * weights[None], axis=1)]
  transfers between devices with their start and end apart: 6 -> 0, of which waited for: 4 -> 0; matrix products, arithmetic and copies ran while one was open for 1% -> 0% of each run, Pallas kernels for 0% -> 0%
where the time goes in v1:
time: 83.2 us; the launch traced here: 82.9 us
  Pallas kernels  74.2 us (89%)
  local copies, waits for them, and re-layouts  8.05 us (10%)
    pallas_call x1, Pallas kernels, shards(): pl.pallas_call(functools.partial(kernel, members, spaces), out_shape=(jax...  74.2 us
    unnamed x16, local copies, waits for them, and re-layouts  8.05 us

profile of v1, /device:TPU:1, one launch (start us, length us, event | category | flops | bytes accessed | tf_op | source)
XLA Modules:
  0.0 82.9 jit_solution(10183193267909055043)
XLA Ops:
  0.6 0.0 copy-start
  0.6 1.1 %copy-done = f32[1,3,65536]{2,0,1:T(1,128)S(1)} copy-done((f32[1,3,65536]{2,0,1:T(1,128)S(1)}, f32[1,3,65536]{2,0,1:T(1,128)}, u32[]{:S(2)}) %copy-start) | copy-done | bytes 786456
  1.8 0.0 copy-start.1
  1.8 1.0 %copy-done.1 = f32[1,4,2,16384]{3,2,1,0:T(2,128)S(1)} copy-done((f32[1,4,2,16384]{3,2,1,0:T(2,128)S(1)}, f32[1,4,2,16384]{3,2,1,0:T(2,128)}, u32[]{:S(2)}) %copy-start.1) | copy-done | bytes 524312
  2.8 0.0 copy-start.2
  2.8 0.9 %copy-done.2 = s32[1,65536]{1,0:T(1,128)S(1)} copy-done((s32[1,65536]{1,0:T(1,128)S(1)}, s32[1,65536]{1,0:T(1,128)}, u32[]{:S(2)}) %copy-start.2) | copy-done | bytes 262168
  3.8 0.0 copy-start.3
  3.8 0.9 %copy-done.3 = s32[1,65536]{1,0:T(1,128)S(1)} copy-done((s32[1,65536]{1,0:T(1,128)S(1)}, s32[1,65536]{1,0:T(1,128)}, u32[]{:S(2)}) %copy-start.3) | copy-done | bytes 262168
  4.7 0.0 copy-start.4
  4.7 0.9 %copy-done.4 = f32[2,16384]{1,0:T(2,128)S(1)} copy-done((f32[2,16384]{1,0:T(2,128)S(1)}, f32[2,16384]{1,0:T(2,128)}, u32[]{:S(2)}) %copy-start.4) | copy-done | bytes 131096
  5.6 0.0 copy-start.5
  5.6 0.8 %copy-done.5 = f32[16384]{0:T(1024)S(1)} copy-done((f32[16384]{0:T(1024)S(1)}, f32[16384]{0:T(1024)}, u32[]{:S(2)}) %copy-start.5) | copy-done | bytes 65560
  6.5 0.0 copy-start.6
  6.5 0.8 %copy-done.6 = f32[16384]{0:T(1024)S(1)} copy-done((f32[16384]{0:T(1024)S(1)}, f32[16384]{0:T(1024)}, u32[]{:S(2)}) %copy-start.6) | copy-done | bytes 65560
  7.3 74.2 %shard_map.86 = (f32[4,256,128]{2,1,0:T(8,128)S(1)}, f32[32,32]{1,0:T(8,128)S(1)}) custom-call(f32[4,256,128]{2,1,0:T(8,128)S(1)} %bitcast.22, f32[256,128]{1,0:T(8,128)S(1)} %bitcast.25, s32[512,128]{1,0:T(8,128)S(1)} %bitcast.23, s32[512,128]{1,0:T(8,128)S(1)} %bitcast.24, f32[3,512,128]{2,1,0:T(8,128)S(1)} %bitcast.20, f32[128,128]{1,0:T(8,128)S(1)} %bitcast.26, ...), custom_call_target="tpu_custom_call" | custom-call | tf_op jit(solution)/shard_map/pallas_call | solution.py:379
  81.5 0.8 copy.14
  82.3 0.6 copy.15
Async XLA Ops:
  0.6 1.1 %copy-start = (f32[1,3,65536]{2,0,1:T(1,128)S(1)}, f32[1,3,65536]{2,0,1:T(1,128)}, u32[]{:S(2)}) copy-start(f32[1,3,65536]{2,0,1:T(1,128)} %param.11) | copy-start | bytes 2359300
  1.8 1.0 %copy-start.1 = (f32[1,4,2,16384]{3,2,1,0:T(2,128)S(1)}, f32[1,4,2,16384]{3,2,1,0:T(2,128)}, u32[]{:S(2)}) copy-start(f32[1,4,2,16384]{3,2,1,0:T(2,128)} %param.7) | copy-start | bytes 1572868
  2.8 0.9 %copy-start.2 = (s32[1,65536]{1,0:T(1,128)S(1)}, s32[1,65536]{1,0:T(1,128)}, u32[]{:S(2)}) copy-start(s32[1,65536]{1,0:T(1,128)} %param.9) | copy-start | bytes 786436
  3.8 0.9 %copy-start.3 = (s32[1,65536]{1,0:T(1,128)S(1)}, s32[1,65536]{1,0:T(1,128)}, u32[]{:S(2)}) copy-start(s32[1,65536]{1,0:T(1,128)} %param.10) | copy-start | bytes 786436
  4.7 0.9 %copy-start.4 = (f32[2,16384]{1,0:T(2,128)S(1)}, f32[2,16384]{1,0:T(2,128)}, u32[]{:S(2)}) copy-start(f32[2,16384]{1,0:T(2,128)} %param.8) | copy-start | bytes 393220
  5.6 0.8 %copy-start.5 = (f32[16384]{0:T(1024)S(1)}, f32[16384]{0:T(1024)}, u32[]{:S(2)}) copy-start(f32[16384]{0:T(1024)} %param.12) | copy-start | bytes 196612
  6.5 0.8 %copy-start.6 = (f32[16384]{0:T(1024)S(1)}, f32[16384]{0:T(1024)}, u32[]{:S(2)}) copy-start(f32[16384]{0:T(1024)} %param.13) | copy-start | bytes 196612

commit v2 on v1

v2 whole, which is shorter than its diff:
```python
import functools

import jax
import jax.numpy as jnp
from jax import lax
from jax.experimental import pallas as pl
from jax.experimental.pallas import tpu as pltpu
from jax.sharding import PartitionSpec as P

NS_STEPS = 8
COURANT = 0.5
BUOYANCY = 0.2
FIELDS = 4
LANES = 128
HALF = 64
BEAM_ROWS = 64
BEAM_COLS = 256
PARTS = 2
LINES = 128
BATCH = 16
BATCHES = LINES // BATCH
MESH = pl.DeviceIdType.MESH
F32 = jnp.float32
BF16 = jnp.bfloat16
HIGHEST = lax.Precision.HIGHEST


def bf16_iota(shape, dim):
    return lax.broadcasted_iota(jnp.int32, shape, dim).astype(F32).astype(BF16)


def stencil(center, behind, ahead, viscous):
    lane = lax.broadcasted_iota(jnp.int32, center.shape, 1)
    depth = lane & (HALF - 1)
    rows = center.shape[0]
    swapped = pltpu.roll(center, HALF, 1)
    lateral = swapped + jnp.where(
        lane < HALF, pltpu.roll(swapped, 1, 0), pltpu.roll(swapped, rows - 1, 0)
    )
    above = jnp.where(depth == HALF - 1, 0.0, pltpu.roll(center, LANES - 1, 1))
    below = jnp.where(depth == 0, 0.0, pltpu.roll(center, 1, 1))
    laplace = behind + ahead + lateral + (above + below) - 6.0 * center
    return center - COURANT * (center - behind) + viscous * laplace


def kernel(
    members, spaces,
    fields_hbm, visc_hbm, cell_hbm, beam_hbm, weight_hbm, observed_hbm, variance_hbm,
    out_ref, mixing_ref,
    fields_ref, visc_ref, cell_ref, beam_ref, weight_ref, observed_ref, variance_ref,
    own, low, high, forecast, pointwise, sight, pair_sight, columns, scatter,
    beam_send, beam_recv, share, gathered, stats_send, stats_recv, mixed, returned,
    load_sem, halo_send_sem, halo_recv_sem, sight_send_sem, sight_recv_sem,
    there_send_sem, there_recv_sem, beam_send_sem, beam_recv_sem,
    gather_send_sem, gather_recv_sem, stats_send_sem, stats_recv_sem, back_send_sem, back_recv_sem,
):
    me = lax.axis_index("member")
    here = lax.axis_index("space")
    core = lax.rem(me, 2)
    pair = me + 1 - 2 * core
    nxt = lax.rem(here + 1, spaces)
    prv = lax.rem(here + spaces - 1, spaces)

    loads = [
        pltpu.make_async_copy(fields_hbm, fields_ref, load_sem.at[0]),
        pltpu.make_async_copy(visc_hbm, visc_ref, load_sem.at[1]),
        pltpu.make_async_copy(beam_hbm, beam_ref, load_sem.at[2]),
        pltpu.make_async_copy(cell_hbm, cell_ref, load_sem.at[3]),
        pltpu.make_async_copy(weight_hbm, weight_ref, load_sem.at[4]),
        pltpu.make_async_copy(observed_hbm, observed_ref, load_sem.at[5]),
        pltpu.make_async_copy(variance_hbm, variance_ref, load_sem.at[6]),
    ]
    for load in loads:
        load.start()

    def others(count, mine, act):
        def one(d, carry):
            act(lax.rem(mine + d, count))
            return carry

        lax.fori_loop(1, count, one, 0)

    barrier = pltpu.get_barrier_semaphore()

    def greet(member, space):
        pl.semaphore_signal(barrier, inc=1, device_id=(member, space), device_id_type=MESH)

    others(spaces, here, lambda t: greet(me, t))
    others(spaces, here, lambda t: greet(pair, t))
    others(members, me, lambda p: greet(p, here))

    loads[0].wait()
    loads[1].wait()

    def spread(source, parity, plane):
        for first, start, count in ((0, LINES - 8, 8), (8, 0, LINES), (LINES + 8, 0, 8)):
            own[plane, pl.ds(first, count), :] = source[pl.ds(2 * start + parity, count, stride=2), :]

    for r in range(2):
        for f in range(FIELDS):
            spread(fields_ref.at[f], r, 1 + FIELDS * r + f)
        spread(visc_ref, r, 9 * r)
    pl.semaphore_wait(barrier, members + 2 * spaces - 3)

    def halo(n):
        lines = pl.ds(pl.multiple_of(BATCH * n, BATCH), BATCH)
        down = pltpu.make_async_remote_copy(
            src_ref=own.at[pl.ds(0, 9), lines], dst_ref=high.at[:, lines],
            send_sem=halo_send_sem.at[0, n], recv_sem=halo_recv_sem.at[0, n],
            device_id=(me, prv), device_id_type=MESH,
        )
        up = pltpu.make_async_remote_copy(
            src_ref=own.at[pl.ds(1, 9), lines], dst_ref=low.at[:, lines],
            send_sem=halo_send_sem.at[1, n], recv_sem=halo_recv_sem.at[1, n],
            device_id=(me, nxt), device_id_type=MESH,
        )
        return down, up

    def start_halo(n, carry):
        for copy in halo(n):
            copy.start()
        return carry

    lax.fori_loop(0, BATCHES, start_halo, 0)

    loads[2].wait()

    def fill_columns(k, carry):
        rows = pl.ds(pl.multiple_of(256 * core + 16 * k, 16), 16)
        beam_col = (beam_ref[rows, :] & (BEAM_COLS - 1)).astype(F32).astype(BF16)
        ids = bf16_iota((BEAM_COLS, LANES), 0)
        ones, zeros = jnp.ones((BEAM_COLS, LANES), BF16), jnp.zeros((BEAM_COLS, LANES), BF16)
        for g in range(16):
            columns[k, g * LANES : (g + 1) * LANES, :] = jnp.where(
                ids == beam_col[g : g + 1], ones, zeros
            ).T
        return carry

    lax.fori_loop(0, 2 * BATCHES, fill_columns, 0)
    for load in loads[3:]:
        load.wait()

    def step_batch(n):
        lines = pl.ds(pl.multiple_of(BATCH * n, BATCH), 2 * BATCH)
        viscous = [low[8, lines], own[0, lines], own[9, lines], high[0, lines]]
        for group in ((2, 3), (0,), (1,)):
            rows = {
                f: [low[f, lines], low[4 + f, lines], own[1 + f, lines],
                    own[5 + f, lines], high[1 + f, lines], high[5 + f, lines]]
                for f in group
            }
            for depth in (4, 2):
                nu = viscous if depth == 4 else viscous[1:3]
                after = {
                    f: [
                        stencil(rows[f][i + 1], rows[f][i], rows[f][i + 2], nu[i])
                        for i in range(depth)
                    ]
                    for f in group
                }
                if len(group) == 2:
                    lift, heat = group
                    after[lift] = [
                        after[lift][i] + BUOYANCY * rows[heat][i + 1] for i in range(depth)
                    ]
                    after[heat] = [
                        after[heat][i] - BUOYANCY * rows[lift][i + 1] for i in range(depth)
                    ]
                rows = after
            for f in group:
                for r in range(2):
                    for h in range(2):
                        block = members // 2 * r + 2 * n + h
                        forecast[block, f] = rows[f][r][8 + 8 * h : 16 + 8 * h]

    def gather_batch(n):
        for r in range(2):
            for h in range(2):
                block = members // 2 * r + 2 * n + h
                for g in range(2):
                    rows = pl.ds(pl.multiple_of(16 * block + 8 * g, 8), 8)
                    cells = cell_ref[rows, :]
                    lane, line = cells & (LANES - 1), cells >> 7
                    total = None
                    for c in range(3):
                        table = forecast[block, c]
                        value = None
                        for t in range(8):
                            row = jnp.broadcast_to(table[t : t + 1], (8, LANES))
                            found = jnp.take_along_axis(
                                row, lane, axis=1, mode="promise_in_bounds"
                            )
                            value = found if value is None else jnp.where(line == t, found, value)
                        term = weight_ref[c, rows, :] * value
                        total = term if total is None else total + term
                    sight[r, n, 16 * h + 8 * g : 16 * h + 8 * g + 8, :] = total

    def pair_copy(n):
        return pltpu.make_async_remote_copy(
            src_ref=sight.at[1 - core, n], dst_ref=pair_sight.at[n],
            send_sem=sight_send_sem.at[n], recv_sem=sight_recv_sem.at[n],
            device_id=(pair, here), device_id_type=MESH,
        )

    def scatter_batch(n):
        ids = bf16_iota((BEAM_ROWS, LANES), 0)
        zeros = jnp.zeros((BEAM_ROWS, LANES), BF16)
        product = None
        for h in range(2):
            parts = []
            for rest in (
                sight[core, n, 16 * h : 16 * h + 16, :], pair_sight[n, 16 * h : 16 * h + 16, :]
            ):
                for _ in range(PARTS):
                    part = rest.astype(BF16)
                    parts.append(part)
                    rest = rest - part.astype(F32)
            rows = pl.ds(pl.multiple_of(256 * core + 32 * n + 16 * h, 16), 16)
            beam_row = (beam_ref[rows, :] >> 8).astype(F32).astype(BF16)
            left = []
            for g in range(16):
                hit = ids == beam_row[g : g + 1]
                left.append(jnp.concatenate([
                    jnp.where(hit, jnp.broadcast_to(part[g : g + 1], (BEAM_ROWS, LANES)), zeros)
                    for part in parts
                ], axis=0))
            term = jnp.dot(
                jnp.concatenate(left, axis=1), columns[2 * n + h], preferred_element_type=F32
            )
            product = term if product is None else product + term
        scatter[...] += product

    def there(p):
        return pltpu.make_async_remote_copy(
            src_ref=forecast.at[p], dst_ref=pointwise.at[me],
            send_sem=there_send_sem.at[p], recv_sem=there_recv_sem.at[me],
            device_id=(p, here), device_id_type=MESH,
        )

    def there_from(i):
        return pltpu.make_async_remote_copy(
            src_ref=forecast.at[i], dst_ref=pointwise.at[i],
            send_sem=there_send_sem.at[i], recv_sem=there_recv_sem.at[i],
            device_id=(i, here), device_id_type=MESH,
        )

    scatter[...] = jnp.zeros_like(scatter)

    def finish_halo(n):
        for copy in halo(n):
            copy.wait_recv()

    finish_halo(0)
    for buffer in (low, high):
        buffer[:, LINES : LINES + BATCH, :] = buffer[:, 0:BATCH, :]
    finish_halo(1)
    step_batch(0)
    gather_batch(0)
    pair_copy(0).start()

    def batch(n, carry):
        @pl.when(n < BATCHES - 1)
        def _():
            finish_halo(n + 1)

        step_batch(n)
        pair_copy(n - 1).wait_recv()
        scatter_batch(n - 1)
        gather_batch(n)
        pair_copy(n).start()
        return carry

    lax.fori_loop(1, BATCHES, batch, 0)
    pair_copy(BATCHES - 1).wait_recv()
    scatter_batch(BATCHES - 1)
    for half in range(2):
        first = 2 * BEAM_ROWS * half
        total = scatter[first : first + BEAM_ROWS] + scatter[first + BEAM_ROWS : first + 2 * BEAM_ROWS]
        beam_send[half] = total.reshape(beam_send.shape[1:])

    def beam_to(half, t):
        return pltpu.make_async_remote_copy(
            src_ref=beam_send.at[half, t], dst_ref=beam_recv.at[half, here],
            send_sem=beam_send_sem.at[half, t], recv_sem=beam_recv_sem.at[half, here],
            device_id=(pair if half else me, t), device_id_type=MESH,
        )

    def beam_from(half, t):
        return pltpu.make_async_remote_copy(
            src_ref=beam_send.at[half, t], dst_ref=beam_recv.at[half, t],
            send_sem=beam_send_sem.at[half, t], recv_sem=beam_recv_sem.at[half, t],
            device_id=(pair if half else me, t), device_id_type=MESH,
        )

    others(spaces, here, lambda t: beam_to(0, t).start())
    others(spaces, here, lambda t: beam_to(1, t).start())
    beam_to(1, here).start()
    beam_recv[0, here] = beam_send[0, here]
    others(members, me, lambda p: there(p).start())
    pointwise[me] = forecast[me]
    beam_from(1, here).wait_recv()
    others(spaces, here, lambda t: beam_from(0, t).wait_recv())
    others(spaces, here, lambda t: beam_from(1, t).wait_recv())
    predicted = beam_recv[0, 0] + beam_recv[1, 0]
    for t in range(1, spaces):
        predicted = predicted + (beam_recv[0, t] + beam_recv[1, t])

    for half in range(2):
        share[half] = predicted[:, half * LANES : (half + 1) * LANES]

    def slot(i):
        return gathered.at[pl.ds(pl.multiple_of(8 * i, 8), 8), :]

    def share_to(p):
        return pltpu.make_async_remote_copy(
            src_ref=share.at[lax.rem(p, 2)], dst_ref=slot(me),
            send_sem=gather_send_sem.at[p], recv_sem=gather_recv_sem.at[me],
            device_id=(p, here), device_id_type=MESH,
        )

    def share_from(i):
        return pltpu.make_async_remote_copy(
            src_ref=share.at[core], dst_ref=slot(i),
            send_sem=gather_send_sem.at[i], recv_sem=gather_recv_sem.at[i],
            device_id=(i, here), device_id_type=MESH,
        )

    others(members, me, lambda p: share_to(p).start())
    gathered[pl.ds(pl.multiple_of(8 * me, 8), 8), :] = share[core]
    others(members, me, lambda i: share_from(i).wait_recv())

    every = jnp.concatenate(
        [gathered[pl.ds(sub, members, stride=8), :] for sub in range(8)], axis=1
    )
    mine = pl.ds(pl.multiple_of(16 * here, 16), 16)

    def core_rows(ref):
        rows = ref[mine, :]
        return jnp.concatenate([
            jnp.where(core == 0, rows[2 * i : 2 * i + 1], rows[2 * i + 1 : 2 * i + 2])
            for i in range(8)
        ], axis=1)

    seen, variance = core_rows(observed_ref), core_rows(variance_ref)
    mean_pred = jnp.mean(every, axis=0, keepdims=True)
    anomaly = every - mean_pred
    scaled = anomaly / variance
    member_id = lax.broadcasted_iota(jnp.int32, anomaly.shape, 0)
    against = jnp.where(member_id == members - 1, seen - mean_pred, anomaly)
    partial = lax.dot_general(
        scaled, against, (((1,), (1,)), ((), ())), precision=HIGHEST, preferred_element_type=F32
    )
    stats_send[...] = jnp.concatenate([partial[8 * g : 8 * g + 8] for g in range(members // 8)], axis=1)

    def stats_copy(other, t, origin_core, origin):
        return pltpu.make_async_remote_copy(
            src_ref=stats_send, dst_ref=stats_recv.at[origin_core, origin],
            send_sem=stats_send_sem.at[other, t], recv_sem=stats_recv_sem.at[origin_core, origin],
            device_id=(pair if other else me, t), device_id_type=MESH,
        )

    def stats_to(other, t):
        return stats_copy(other, t, core, here)

    def stats_from(other, t):
        return stats_copy(other, t, 1 - core if other else core, t)

    others(spaces, here, lambda t: stats_to(0, t).start())
    others(spaces, here, lambda t: stats_to(1, t).start())
    stats_to(1, here).start()
    stats_recv[core, here] = stats_send[...]
    stats_from(1, here).wait_recv()
    others(spaces, here, lambda t: stats_from(0, t).wait_recv())
    others(spaces, here, lambda t: stats_from(1, t).wait_recv())
    packed = stats_recv[0, 0] + stats_recv[1, 0]
    for t in range(1, spaces):
        packed = packed + (stats_recv[0, t] + stats_recv[1, t])
    stats = jnp.concatenate(
        [packed[:, members * g : members * (g + 1)] for g in range(members // 8)], axis=0
    )

    def times(a, b):
        return jnp.dot(a, b, precision=HIGHEST, preferred_element_type=F32)

    row_id = lax.broadcasted_iota(jnp.int32, (members, members), 0)
    col_id = lax.broadcasted_iota(jnp.int32, (members, members), 1)
    last = col_id == members - 1
    rest = jnp.sum(jnp.where(last, 0.0, stats), axis=1, keepdims=True)
    covar = jnp.where(last, -rest, stats)
    identity = jnp.where(row_id == col_id, 1.0, 0.0).astype(F32)
    system = identity + covar / (members - 1.0)
    magnitude = jnp.sqrt(jnp.sum(system * system, axis=(0, 1), keepdims=True))
    iterate = system / magnitude
    inverse_root = identity
    for _ in range(NS_STEPS):
        factor = 1.5 * identity - 0.5 * times(inverse_root, iterate)
        iterate = times(iterate, factor)
        inverse_root = times(factor, inverse_root)
    root_part = inverse_root / jnp.sqrt(magnitude)
    inverse_full = times(inverse_root, inverse_root) / magnitude
    shift = times(inverse_full, stats)[:, members - 1 : members] / (members - 1.0)
    combined = root_part + shift
    mixing = combined - jnp.mean(combined, axis=0, keepdims=True) + 1.0 / members
    mixing_ref[...] = mixing

    others(members, me, lambda i: there_from(i).wait_recv())
    count = FIELDS * 8
    block = jnp.concatenate(
        [pointwise.reshape(members * count, LANES)[pl.ds(k, members, stride=count), :] for k in range(count)],
        axis=1,
    )
    analysed = lax.dot_general(
        mixing, block, (((0,), (0,)), ((), ())), precision=HIGHEST, preferred_element_type=F32
    )
    for k in range(count):
        mixed.reshape(members * count, LANES)[pl.ds(k, members, stride=count), :] = (
            analysed[:, k * LANES : (k + 1) * LANES]
        )

    def back(j):
        return pltpu.make_async_remote_copy(
            src_ref=mixed.at[j], dst_ref=returned.at[me],
            send_sem=back_send_sem.at[j], recv_sem=back_recv_sem.at[me],
            device_id=(j, here), device_id_type=MESH,
        )

    def back_from(p):
        return pltpu.make_async_remote_copy(
            src_ref=mixed.at[p], dst_ref=returned.at[p],
            send_sem=back_send_sem.at[p], recv_sem=back_recv_sem.at[p],
            device_id=(p, here), device_id_type=MESH,
        )

    others(members, me, lambda j: back(j).start())
    returned[me] = mixed[me]

    def finish_send(n, carry):
        for copy in halo(n):
            copy.wait_send()
        pair_copy(n).wait_send()
        return carry

    lax.fori_loop(0, BATCHES, finish_send, 0)
    others(members, me, lambda p: there(p).wait_send())
    beam_to(1, here).wait_send()
    stats_to(1, here).wait_send()
    for half in range(2):
        others(spaces, here, lambda t: beam_to(half, t).wait_send())
        others(spaces, here, lambda t: stats_to(half, t).wait_send())
    others(members, me, lambda p: share_to(p).wait_send())
    others(members, me, lambda p: back_from(p).wait_recv())
    for p in range(members):
        r, q = divmod(p, members // 2)
        for f in range(FIELDS):
            out_ref[f, pl.ds(16 * q + r, 8, stride=2), :] = returned[p, f]
    others(members, me, lambda j: back(j).wait_send())


def shards(members, spaces, realization_fields, viscosity, cell_index, beam_id, los_weight, observed, obs_variance):
    _, fields, rows, plane = realization_fields.shape
    lines = plane // LANES
    samples = cell_index.shape[1] // LANES
    beams = observed.shape[0] // LANES
    mixed_rows = realization_fields.reshape(fields, rows, lines, LANES).transpose(0, 2, 1, 3)
    visc_rows = viscosity.reshape(rows, lines, LANES).transpose(1, 0, 2)
    block = (members, FIELDS, 8, LANES)
    share = (BEAM_ROWS // spaces, BEAM_COLS)
    dma = lambda *shape: pltpu.SemaphoreType.DMA(shape)
    vmem = pl.BlockSpec(memory_space=pltpu.VMEM)
    analysis, mixing = pl.pallas_call(
        functools.partial(kernel, members, spaces),
        out_shape=(
            jax.ShapeDtypeStruct((fields, rows * lines, LANES), F32),
            jax.ShapeDtypeStruct((members, members), F32),
        ),
        in_specs=[pl.BlockSpec(memory_space=pl.ANY)] * 7,
        out_specs=(vmem, vmem),
        scratch_shapes=[
            pltpu.VMEM((fields, rows * lines, LANES), F32),
            pltpu.VMEM((rows * lines, LANES), F32),
            pltpu.VMEM((samples, LANES), jnp.int32),
            pltpu.VMEM((samples, LANES), jnp.int32),
            pltpu.VMEM((3, samples, LANES), F32),
            pltpu.VMEM((beams, LANES), F32),
            pltpu.VMEM((beams, LANES), F32),
            pltpu.VMEM((10, LINES + BATCH, LANES), F32),
            pltpu.VMEM((9, LINES + BATCH, LANES), F32),
            pltpu.VMEM((9, LINES + BATCH, LANES), F32),
            pltpu.VMEM(block, F32),
            pltpu.VMEM(block, F32),
            pltpu.VMEM((2, BATCHES, 32, LANES), F32),
            pltpu.VMEM((BATCHES, 32, LANES), F32),
            pltpu.VMEM((2 * BATCHES, 16 * LANES, BEAM_COLS), BF16),
            pltpu.VMEM((2 * PARTS * BEAM_ROWS, BEAM_COLS), F32),
            pltpu.VMEM((2, spaces) + share, F32),
            pltpu.VMEM((2, spaces) + share, F32),
            pltpu.VMEM((2, share[0], LANES), F32),
            pltpu.VMEM((members * share[0], LANES), F32),
            pltpu.VMEM((8, LANES), F32),
            pltpu.VMEM((2, spaces, 8, LANES), F32),
            pltpu.VMEM(block, F32),
            pltpu.VMEM(block, F32),
            dma(7),
            dma(2, BATCHES), dma(2, BATCHES),
            dma(BATCHES), dma(BATCHES),
            dma(members), dma(members),
            dma(2, spaces), dma(2, spaces),
            dma(members), dma(members),
            dma(2, spaces), dma(2, spaces),
            dma(members), dma(members),
        ],
        compiler_params=pltpu.CompilerParams(
            collective_id=0, has_side_effects=True, vmem_limit_bytes=60 << 20
        ),
    )(
        mixed_rows.reshape(fields, lines * rows, LANES),
        visc_rows.reshape(lines * rows, LANES),
        cell_index.reshape(samples, LANES),
        beam_id.reshape(samples, LANES),
        los_weight.reshape(3, samples, LANES),
        observed.reshape(beams, LANES),
        obs_variance.reshape(beams, LANES),
    )
    analysis = analysis.reshape(fields, lines, rows, LANES).transpose(0, 2, 1, 3)
    return analysis.reshape(realization_fields.shape), mixing


def solution(mesh):
    return jax.shard_map(
        functools.partial(shards, mesh.shape["member"], mesh.shape["space"]),
        mesh=mesh,
        in_specs=(
            P("member", None, "space", None),
            P("space", None),
            P("space", None),
            P("space", None),
            P("space", None, None),
            P(),
            P(),
        ),
        out_specs=(P("member", None, "space", None), P()),
        check_vma=False,
    )
```

time: 83.2 us -> 69.2 us (0.83)
  Pallas kernels: 74.2 us -> 65.9 us
  local copies, waits for them, and re-layouts: 8.05 us -> 2.48 us
    pallas_call x1, Pallas kernels: 74.2 us -> 65.9 us  [shards(): pl.pallas_call(functools.partial(kernel, members, spaces), out_shape=(jax...]
    unnamed x16 -> x4, local copies, waits for them, and re-layouts: 8.05 us -> 2.48 us
where the time goes in v2:
time: 69.2 us; the launch traced here: 69 us
  Pallas kernels  65.9 us (95%)
  local copies, waits for them, and re-layouts  2.48 us (4%)
    pallas_call x1, Pallas kernels, shards(): pl.pallas_call(functools.partial(kernel, members, spaces), out_shape=(jax...  65.9 us
    unnamed x4, local copies, waits for them, and re-layouts  2.48 us

profile of v2, /device:TPU:1, one launch (start us, length us, event | category | flops | bytes accessed | tf_op | source)
XLA Modules:
  0.0 69.0 jit_solution(638070028990403755)
XLA Ops:
  0.6 65.9 %shard_map.86 = (f32[4,256,128]{2,1,0:T(8,128)}, f32[32,32]{1,0:T(8,128)}) custom-call(f32[4,256,128]{2,1,0:T(8,128)} %bitcast.22, f32[256,128]{1,0:T(8,128)} %bitcast.25, s32[512,128]{1,0:T(8,128)} %bitcast.23, s32[512,128]{1,0:T(8,128)} %bitcast.24, f32[3,512,128]{2,1,0:T(8,128)} %bitcast.20, f32[128,128]{1,0:T(8,128)} %bitcast.26, f32[128,128]{1,0:T(8,128)} %bitcast.27), custom_call_target="tpu_custom_call" | custom-call | tf_op jit(solution)/shard_map/pallas_call | solution.py:470
  66.5 0.0 copy-start
  66.5 1.9 %copy.14 = f32[1,4,2,16384]{3,2,1,0:T(2,128)} copy(f32[1,4,2,16384]{3,2,1,0:T(2,128)} %bitcast.21) | data formatting | bytes 1048576
  68.4 0.0 copy-done
  68.4 0.6 copy.15
Async XLA Ops:
  66.5 1.9 %copy-start = (f32[32,32]{1,0:T(8,128)S(1)}, f32[32,32]{1,0:T(8,128)}, u32[]{:S(2)}) copy-start(f32[32,32]{1,0:T(8,128)} %get-tuple-element.9) | copy-start | bytes 12292

commit v3 on v2

--- a/solution.py
+++ b/solution.py
@@ -19,6 +19,8 @@
 LINES = 128
 BATCH = 16
 BATCHES = LINES // BATCH
+SIDE = 4
+RELAYS = 4
 MESH = pl.DeviceIdType.MESH
 F32 = jnp.float32
 BF16 = jnp.bfloat16
@@ -50,7 +52,7 @@
     fields_ref, visc_ref, cell_ref, beam_ref, weight_ref, observed_ref, variance_ref,
     own, low, high, forecast, pointwise, sight, pair_sight, columns, scatter,
     beam_send, beam_recv, share, gathered, stats_send, stats_recv, mixed, returned,
-    load_sem, halo_send_sem, halo_recv_sem, sight_send_sem, sight_recv_sem,
+    load_sem, relay_sem, halo_send_sem, halo_recv_sem, sight_send_sem, sight_recv_sem,
     there_send_sem, there_recv_sem, beam_send_sem, beam_recv_sem,
     gather_send_sem, gather_recv_sem, stats_send_sem, stats_recv_sem, back_send_sem, back_recv_sem,
 ):
@@ -70,8 +72,6 @@
         pltpu.make_async_copy(observed_hbm, observed_ref, load_sem.at[5]),
         pltpu.make_async_copy(variance_hbm, variance_ref, load_sem.at[6]),
     ]
-    for load in loads:
-        load.start()
 
     def others(count, mine, act):
         def one(d, carry):
@@ -82,12 +82,31 @@
 
     barrier = pltpu.get_barrier_semaphore()
 
-    def greet(member, space):
-        pl.semaphore_signal(barrier, inc=1, device_id=(member, space), device_id_type=MESH)
-
-    others(spaces, here, lambda t: greet(me, t))
-    others(spaces, here, lambda t: greet(pair, t))
-    others(members, me, lambda p: greet(p, here))
+    chip = me // 2
+    across, along = chip // SIDE, lax.rem(chip, SIDE)
+
+    def device_at(x, y):
+        return 2 * (SIDE * lax.rem(x, SIDE) + lax.rem(y, SIDE)) + core
+
+    near = (
+        (me, nxt), (me, prv), (pair, here),
+        (device_at(across + 1, along), here), (device_at(across + SIDE - 1, along), here),
+        (device_at(across, along + 1), here), (device_at(across, along + SIDE - 1), here),
+    )
+
+    def greet(semaphore):
+        for device in near:
+            pl.semaphore_signal(semaphore, inc=1, device_id=device, device_id_type=MESH)
+
+    def hand_on(k):
+        if k > 0:
+            pl.semaphore_wait(relay_sem.at[k - 1], len(near))
+        if k < RELAYS:
+            greet(relay_sem.at[k])
+
+    greet(barrier)
+    for load in loads:
+        load.start()
 
     loads[0].wait()
     loads[1].wait()
@@ -100,7 +119,7 @@
         for f in range(FIELDS):
             spread(fields_ref.at[f], r, 1 + FIELDS * r + f)
         spread(visc_ref, r, 9 * r)
-    pl.semaphore_wait(barrier, members + 2 * spaces - 3)
+    pl.semaphore_wait(barrier, len(near))
 
     def halo(n):
         lines = pl.ds(pl.multiple_of(BATCH * n, BATCH), BATCH)
@@ -116,16 +135,21 @@
         )
         return down, up
 
-    def start_halo(n, carry):
+    def start_halo(n):
         for copy in halo(n):
             copy.start()
-        return carry
-
-    lax.fori_loop(0, BATCHES, start_halo, 0)
+
+    start_halo(0)
+    start_halo(1)
+    hand_on(0)
 
     loads[2].wait()
 
     def fill_columns(k, carry):
+        @pl.when(lax.rem(k, 4) == 0)
+        def _():
+            start_halo(2 + k // 4)
+
         rows = pl.ds(pl.multiple_of(256 * core + 16 * k, 16), 16)
         beam_col = (beam_ref[rows, :] & (BEAM_COLS - 1)).astype(F32).astype(BF16)
         ids = bf16_iota((BEAM_COLS, LANES), 0)
@@ -250,29 +274,78 @@
         for copy in halo(n):
             copy.wait_recv()
 
+    def send_blocks(n):
+        for r in range(2):
+            for h in range(2):
+                block = members // 2 * r + 2 * n + h
+
+                @pl.when(block != me)
+                def _():
+                    there(block).start()
+
+    def scatter_next(n):
+        pair_copy(n).wait_recv()
+        scatter_batch(n)
+
+    def send_blocks(n):
+        for r in range(2):
+            for h in range(2):
+                block = members // 2 * r + 2 * n + h
+
+                @pl.when(block != me)
+                def _():
+                    there(block).start()
+
+    hand_on(1)
     finish_halo(0)
     for buffer in (low, high):
         buffer[:, LINES : LINES + BATCH, :] = buffer[:, 0:BATCH, :]
-    finish_halo(1)
-    step_batch(0)
-    gather_batch(0)
-    pair_copy(0).start()
-
-    def batch(n, carry):
-        @pl.when(n < BATCHES - 1)
-        def _():
-            finish_halo(n + 1)
-
+    for n in range(2):
+        finish_halo(n + 1)
+        start_halo(BATCHES - 2 + n)
         step_batch(n)
-        pair_copy(n - 1).wait_recv()
-        scatter_batch(n - 1)
         gather_batch(n)
         pair_copy(n).start()
+        hand_on(2 + n)
+
+    def batch(n, carry):
+        finish_halo(n + 1)
+        step_batch(n)
+        pair_copy(n - 2).wait_recv()
+        scatter_batch(n - 2)
+        gather_batch(n)
+        pair_copy(n).start()
+
+        @pl.when(n == 2)
+        def _():
+            hand_on(RELAYS)
+
+        @pl.when(n < 4)
+        def _():
+            send_blocks(2 * n - 4)
+            send_blocks(2 * n - 3)
+
+        @pl.when(n >= 4)
+        def _():
+            send_blocks(n)
+
         return carry
 
-    lax.fori_loop(1, BATCHES, batch, 0)
-    pair_copy(BATCHES - 1).wait_recv()
-    scatter_batch(BATCHES - 1)
+    lax.fori_loop(2, BATCHES - 2, batch, 0)
+    scatter_next(BATCHES - 4)
+    finish_halo(BATCHES - 1)
+    step_batch(BATCHES - 2)
+    pair_copy(BATCHES - 3).wait_recv()
+    scatter_batch(BATCHES - 3)
+    gather_batch(BATCHES - 2)
+    pair_copy(BATCHES - 2).start()
+    step_batch(BATCHES - 1)
+    gather_batch(BATCHES - 1)
+    pair_copy(BATCHES - 1).start()
+    send_blocks(BATCHES - 2)
+    send_blocks(BATCHES - 1)
+    scatter_next(BATCHES - 2)
+    scatter_next(BATCHES - 1)
     for half in range(2):
         first = 2 * BEAM_ROWS * half
         total = scatter[first : first + BEAM_ROWS] + scatter[first + BEAM_ROWS : first + 2 * BEAM_ROWS]
@@ -296,7 +369,6 @@
     others(spaces, here, lambda t: beam_to(1, t).start())
     beam_to(1, here).start()
     beam_recv[0, here] = beam_send[0, here]
-    others(members, me, lambda p: there(p).start())
     pointwise[me] = forecast[me]
     beam_from(1, here).wait_recv()
     others(spaces, here, lambda t: beam_from(0, t).wait_recv())
@@ -500,7 +572,7 @@
             pltpu.VMEM((2, spaces, 8, LANES), F32),
             pltpu.VMEM(block, F32),
             pltpu.VMEM(block, F32),
-            dma(7),
+            dma(7), pltpu.SemaphoreType.REGULAR((RELAYS,)),
             dma(2, BATCHES), dma(2, BATCHES),
             dma(BATCHES), dma(BATCHES),
             dma(members), dma(members),

time: 69.2 us -> 67.4 us (0.974)
  Pallas kernels: 65.9 us -> 64.2 us
    pallas_call x1, Pallas kernels: 65.9 us -> 64.2 us  [shards(): pl.pallas_call(functools.partial(kernel, members, spaces), out_shape=(jax...]
where the time goes in v3:
time: 67.4 us; the launch traced here: 67.3 us
  Pallas kernels  64.2 us (95%)
  local copies, waits for them, and re-layouts  2.48 us (4%)
    pallas_call x1, Pallas kernels, shards(): pl.pallas_call(functools.partial(kernel, members, spaces), out_shape=(jax...  64.2 us
    unnamed x4, local copies, waits for them, and re-layouts  2.48 us

profile of v3, /device:TPU:1, one launch (start us, length us, event | category | flops | bytes accessed | tf_op | source)
XLA Modules:
  0.0 67.3 jit_solution(12583629963086941820)
XLA Ops:
  0.6 64.2 %shard_map.86 = (f32[4,256,128]{2,1,0:T(8,128)}, f32[32,32]{1,0:T(8,128)}) custom-call(f32[4,256,128]{2,1,0:T(8,128)} %bitcast.22, f32[256,128]{1,0:T(8,128)} %bitcast.25, s32[512,128]{1,0:T(8,128)} %bitcast.23, s32[512,128]{1,0:T(8,128)} %bitcast.24, f32[3,512,128]{2,1,0:T(8,128)} %bitcast.20, f32[128,128]{1,0:T(8,128)} %bitcast.26, f32[128,128]{1,0:T(8,128)} %bitcast.27), custom_call_target="tpu_custom_call" | custom-call | tf_op jit(solution)/shard_map/pallas_call | solution.py:542
  64.8 0.0 copy-start
  64.8 1.9 %copy.14 = f32[1,4,2,16384]{3,2,1,0:T(2,128)} copy(f32[1,4,2,16384]{3,2,1,0:T(2,128)} %bitcast.21) | data formatting | bytes 1048576
  66.7 0.0 copy-done
  66.7 0.6 copy.15
Async XLA Ops:
  64.8 1.9 %copy-start = (f32[32,32]{1,0:T(8,128)S(1)}, f32[32,32]{1,0:T(8,128)}, u32[]{:S(2)}) copy-start(f32[32,32]{1,0:T(8,128)} %get-tuple-element.9) | copy-start | bytes 12292

commit v4 on v2

--- a/solution.py
+++ b/solution.py
@@ -19,14 +19,36 @@
 LINES = 128
 BATCH = 16
 BATCHES = LINES // BATCH
+LAG = 2
+SIDE = 4
+RELAYS = 4
 MESH = pl.DeviceIdType.MESH
 F32 = jnp.float32
 BF16 = jnp.bfloat16
-HIGHEST = lax.Precision.HIGHEST
 
 
 def bf16_iota(shape, dim):
     return lax.broadcasted_iota(jnp.int32, shape, dim).astype(F32).astype(BF16)
+
+
+def split(values, count):
+    parts = []
+    for _ in range(count):
+        parts.append(values.astype(BF16))
+        values = values - parts[-1].astype(F32)
+    return parts
+
+
+def times(a, b):
+    a0, a1, a2 = split(a, 3)
+    b0, b1, b2 = split(b, 3)
+    n = a.shape[0]
+    dot = functools.partial(jnp.dot, preferred_element_type=F32)
+    first = dot(jnp.concatenate([a0, a1, a2], axis=0), b0)
+    second = dot(jnp.concatenate([a0, a1], axis=0), b1)
+    third = dot(a0, b2)
+    small = second[n:] + (first[2 * n :] + third)
+    return first[:n] + ((first[n : 2 * n] + second[:n]) + small)
 
 
 def stencil(center, behind, ahead, viscous):
@@ -50,7 +72,7 @@
     fields_ref, visc_ref, cell_ref, beam_ref, weight_ref, observed_ref, variance_ref,
     own, low, high, forecast, pointwise, sight, pair_sight, columns, scatter,
     beam_send, beam_recv, share, gathered, stats_send, stats_recv, mixed, returned,
-    load_sem, halo_send_sem, halo_recv_sem, sight_send_sem, sight_recv_sem,
+    load_sem, relay_sem, halo_send_sem, halo_recv_sem, sight_send_sem, sight_recv_sem,
     there_send_sem, there_recv_sem, beam_send_sem, beam_recv_sem,
     gather_send_sem, gather_recv_sem, stats_send_sem, stats_recv_sem, back_send_sem, back_recv_sem,
 ):
@@ -70,24 +92,54 @@
         pltpu.make_async_copy(observed_hbm, observed_ref, load_sem.at[5]),
         pltpu.make_async_copy(variance_hbm, variance_ref, load_sem.at[6]),
     ]
+
+    chip = me // 2
+    across, along = chip // SIDE, lax.rem(chip, SIDE)
+
+    def device_at(x, y, side):
+        return 2 * (SIDE * lax.rem(x, SIDE) + lax.rem(y, SIDE)) + side
+
+    def ring(i):
+        return lax.rem(6 - i + jnp.where(i >= 2, 7 - 2 * i, 0), SIDE)
+
+    def other_members(act):
+        def one(i, carry):
+            flip = 1 - lax.rem(i, 2)
+            side = core + flip - 2 * core * flip
+            act(device_at(across + ring(i // 8), along + ring(lax.rem(i // 2, SIDE)), side))
+            return carry
+
+        lax.fori_loop(0, members - 1, one, 0)
+
+    def other_spaces(act):
+        def one(j, carry):
+            step = (j + 1) // 2
+            act(lax.rem(here + spaces // 2 + jnp.where(lax.rem(j, 2) == 1, spaces - step, step), spaces))
+            return carry
+
+        lax.fori_loop(0, spaces - 1, one, 0)
+
+    barrier = pltpu.get_barrier_semaphore()
+
+    near = (
+        (me, nxt), (me, prv), (pair, here),
+        (device_at(across + 1, along, core), here), (device_at(across + SIDE - 1, along, core), here),
+        (device_at(across, along + 1, core), here), (device_at(across, along + SIDE - 1, core), here),
+    )
+
+    def greet(semaphore):
+        for device in near:
+            pl.semaphore_signal(semaphore, inc=1, device_id=device, device_id_type=MESH)
+
+    def hand_on(k):
+        if k > 0:
+            pl.semaphore_wait(relay_sem.at[k - 1], len(near))
+        if k < RELAYS:
+            greet(relay_sem.at[k])
+
+    greet(barrier)
     for load in loads:
         load.start()
-
-    def others(count, mine, act):
-        def one(d, carry):
-            act(lax.rem(mine + d, count))
-            return carry
-
-        lax.fori_loop(1, count, one, 0)
-
-    barrier = pltpu.get_barrier_semaphore()
-
-    def greet(member, space):
-        pl.semaphore_signal(barrier, inc=1, device_id=(member, space), device_id_type=MESH)
-
-    others(spaces, here, lambda t: greet(me, t))
-    others(spaces, here, lambda t: greet(pair, t))
-    others(members, me, lambda p: greet(p, here))
 
     loads[0].wait()
     loads[1].wait()
@@ -96,11 +148,15 @@
         for first, start, count in ((0, LINES - 8, 8), (8, 0, LINES), (LINES + 8, 0, 8)):
             own[plane, pl.ds(first, count), :] = source[pl.ds(2 * start + parity, count, stride=2), :]
 
+    def spread_field(f, carry):
+        for r in range(2):
+            spread(fields_ref.at[f], r, 1 + FIELDS * r + f)
+        return carry
+
+    lax.fori_loop(0, FIELDS, spread_field, 0)
     for r in range(2):
-        for f in range(FIELDS):
-            spread(fields_ref.at[f], r, 1 + FIELDS * r + f)
         spread(visc_ref, r, 9 * r)
-    pl.semaphore_wait(barrier, members + 2 * spaces - 3)
+    pl.semaphore_wait(barrier, len(near))
 
     def halo(n):
         lines = pl.ds(pl.multiple_of(BATCH * n, BATCH), BATCH)
@@ -116,27 +172,32 @@
         )
         return down, up
 
-    def start_halo(n, carry):
+    def start_halo(n):
         for copy in halo(n):
             copy.start()
-        return carry
-
-    lax.fori_loop(0, BATCHES, start_halo, 0)
+
+    start_halo(0)
+    start_halo(1)
+    hand_on(0)
 
     loads[2].wait()
 
     def fill_columns(k, carry):
-        rows = pl.ds(pl.multiple_of(256 * core + 16 * k, 16), 16)
+        @pl.when(lax.rem(k, 8) == 0)
+        def _():
+            start_halo(2 + k // 8)
+
+        rows = pl.ds(pl.multiple_of(256 * core + 8 * k, 8), 8)
         beam_col = (beam_ref[rows, :] & (BEAM_COLS - 1)).astype(F32).astype(BF16)
         ids = bf16_iota((BEAM_COLS, LANES), 0)
         ones, zeros = jnp.ones((BEAM_COLS, LANES), BF16), jnp.zeros((BEAM_COLS, LANES), BF16)
-        for g in range(16):
+        for g in range(8):
             columns[k, g * LANES : (g + 1) * LANES, :] = jnp.where(
                 ids == beam_col[g : g + 1], ones, zeros
             ).T
         return carry
 
-    lax.fori_loop(0, 2 * BATCHES, fill_columns, 0)
+    lax.fori_loop(0, 4 * BATCHES, fill_columns, 0)
     for load in loads[3:]:
         load.wait()
 
@@ -174,9 +235,10 @@
                         forecast[block, f] = rows[f][r][8 + 8 * h : 16 + 8 * h]
 
     def gather_batch(n):
+        slot = lax.min(n, BATCHES)
         for r in range(2):
             for h in range(2):
-                block = members // 2 * r + 2 * n + h
+                block = members // 2 * r + 2 * lax.min(n, BATCHES - 1) + h
                 for g in range(2):
                     rows = pl.ds(pl.multiple_of(16 * block + 8 * g, 8), 8)
                     cells = cell_ref[rows, :]
@@ -193,7 +255,7 @@
                             value = found if value is None else jnp.where(line == t, found, value)
                         term = weight_ref[c, rows, :] * value
                         total = term if total is None else total + term
-                    sight[r, n, 16 * h + 8 * g : 16 * h + 8 * g + 8, :] = total
+                    sight[r, slot, 16 * h + 8 * g : 16 * h + 8 * g + 8, :] = total
 
     def pair_copy(n):
         return pltpu.make_async_remote_copy(
@@ -205,30 +267,22 @@
     def scatter_batch(n):
         ids = bf16_iota((BEAM_ROWS, LANES), 0)
         zeros = jnp.zeros((BEAM_ROWS, LANES), BF16)
-        product = None
+        left = []
         for h in range(2):
-            parts = []
-            for rest in (
-                sight[core, n, 16 * h : 16 * h + 16, :], pair_sight[n, 16 * h : 16 * h + 16, :]
-            ):
-                for _ in range(PARTS):
-                    part = rest.astype(BF16)
-                    parts.append(part)
-                    rest = rest - part.astype(F32)
+            lines = slice(16 * h, 16 * h + 16)
+            parts = split(sight[core, n, lines, :], PARTS) + split(pair_sight[n, lines, :], PARTS)
             rows = pl.ds(pl.multiple_of(256 * core + 32 * n + 16 * h, 16), 16)
             beam_row = (beam_ref[rows, :] >> 8).astype(F32).astype(BF16)
-            left = []
             for g in range(16):
                 hit = ids == beam_row[g : g + 1]
                 left.append(jnp.concatenate([
                     jnp.where(hit, jnp.broadcast_to(part[g : g + 1], (BEAM_ROWS, LANES)), zeros)
                     for part in parts
                 ], axis=0))
-            term = jnp.dot(
-                jnp.concatenate(left, axis=1), columns[2 * n + h], preferred_element_type=F32
-            )
-            product = term if product is None else product + term
-        scatter[...] += product
+        right = columns[pl.ds(4 * n, 4)].reshape(32 * LANES, BEAM_COLS)
+        scatter[...] += jnp.dot(
+            jnp.concatenate(left, axis=1), right, preferred_element_type=F32
+        )
 
     def there(p):
         return pltpu.make_async_remote_copy(
@@ -250,29 +304,74 @@
         for copy in halo(n):
             copy.wait_recv()
 
+    def send_blocks(n):
+        for r in range(2):
+            for h in range(2):
+                block = members // 2 * r + 2 * n + h
+
+                @pl.when(block != me)
+                def _():
+                    there(block).start()
+
+    hand_on(1)
     finish_halo(0)
     for buffer in (low, high):
         buffer[:, LINES : LINES + BATCH, :] = buffer[:, 0:BATCH, :]
-    finish_halo(1)
-    step_batch(0)
-    gather_batch(0)
-    pair_copy(0).start()
+
+    def first_batch(n, carry):
+        finish_halo(n + 1)
+        start_halo(BATCHES - LAG + n)
+        step_batch(n)
+        gather_batch(n)
+        pair_copy(n).start()
+        for k in range(LAG):
+            @pl.when(n == k)
+            def _():
+                hand_on(2 + k)
+
+        return carry
 
     def batch(n, carry):
         @pl.when(n < BATCHES - 1)
         def _():
             finish_halo(n + 1)
 
-        step_batch(n)
-        pair_copy(n - 1).wait_recv()
-        scatter_batch(n - 1)
+        @pl.when(n < BATCHES)
+        def _():
+            step_batch(n)
+
+        pair_copy(n - LAG).wait_recv()
+        scatter_batch(n - LAG)
         gather_batch(n)
-        pair_copy(n).start()
+
+        @pl.when(n < BATCHES)
+        def _():
+            pair_copy(n).start()
+
+        @pl.when(n == LAG)
+        def _():
+            hand_on(RELAYS)
+
+        def send_row(r, inner):
+            def send_block(h, inner):
+                block = members // 2 * r + 4 * (n - BATCHES // 2) + h
+
+                @pl.when(block != me)
+                def _():
+                    there(block).start()
+
+                return inner
+
+            return lax.fori_loop(0, 4, send_block, inner)
+
+        @pl.when(jnp.logical_and(n >= BATCHES // 2, n < BATCHES))
+        def _():
+            lax.fori_loop(0, 2, send_row, 0)
+
         return carry
 
-    lax.fori_loop(1, BATCHES, batch, 0)
-    pair_copy(BATCHES - 1).wait_recv()
-    scatter_batch(BATCHES - 1)
+    lax.fori_loop(0, LAG, first_batch, 0)
+    lax.fori_loop(LAG, BATCHES + LAG, batch, 0)
     for half in range(2):
         first = 2 * BEAM_ROWS * half
         total = scatter[first : first + BEAM_ROWS] + scatter[first + BEAM_ROWS : first + 2 * BEAM_ROWS]
@@ -292,15 +391,17 @@
             device_id=(pair if half else me, t), device_id_type=MESH,
         )
 
-    others(spaces, here, lambda t: beam_to(0, t).start())
-    others(spaces, here, lambda t: beam_to(1, t).start())
+    def send_share(t):
+        beam_to(0, t).start()
+        beam_to(1, t).start()
+
+    other_spaces(send_share)
     beam_to(1, here).start()
     beam_recv[0, here] = beam_send[0, here]
-    others(members, me, lambda p: there(p).start())
     pointwise[me] = forecast[me]
     beam_from(1, here).wait_recv()
-    others(spaces, here, lambda t: beam_from(0, t).wait_recv())
-    others(spaces, here, lambda t: beam_from(1, t).wait_recv())
+    other_spaces(lambda t: beam_from(0, t).wait_recv())
+    other_spaces(lambda t: beam_from(1, t).wait_recv())
     predicted = beam_recv[0, 0] + beam_recv[1, 0]
     for t in range(1, spaces):
         predicted = predicted + (beam_recv[0, t] + beam_recv[1, t])
@@ -325,9 +426,9 @@
             device_id=(i, here), device_id_type=MESH,
         )
 
-    others(members, me, lambda p: share_to(p).start())
+    other_members(lambda p: share_to(p).start())
     gathered[pl.ds(pl.multiple_of(8 * me, 8), 8), :] = share[core]
-    others(members, me, lambda i: share_from(i).wait_recv())
+    other_members(lambda i: share_from(i).wait_recv())
 
     every = jnp.concatenate(
         [gathered[pl.ds(sub, members, stride=8), :] for sub in range(8)], axis=1
@@ -347,9 +448,15 @@
     scaled = anomaly / variance
     member_id = lax.broadcasted_iota(jnp.int32, anomaly.shape, 0)
     against = jnp.where(member_id == members - 1, seen - mean_pred, anomaly)
-    partial = lax.dot_general(
-        scaled, against, (((1,), (1,)), ((), ())), precision=HIGHEST, preferred_element_type=F32
+    product = lax.dot_general(
+        jnp.concatenate(split(scaled, 3), axis=0), jnp.concatenate(split(against, 3), axis=0),
+        (((1,), (1,)), ((), ())), preferred_element_type=F32,
     )
+
+    def term(i, j):
+        return product[members * i : members * (i + 1), members * j : members * (j + 1)]
+
+    partial = term(0, 0) + ((term(0, 1) + term(1, 0)) + (term(1, 1) + (term(0, 2) + term(2, 0))))
     stats_send[...] = jnp.concatenate([partial[8 * g : 8 * g + 8] for g in range(members // 8)], axis=1)
 
     def stats_copy(other, t, origin_core, origin):
@@ -365,22 +472,22 @@
     def stats_from(other, t):
         return stats_copy(other, t, 1 - core if other else core, t)
 
-    others(spaces, here, lambda t: stats_to(0, t).start())
-    others(spaces, here, lambda t: stats_to(1, t).start())
+    def send_stats(t):
+        stats_to(0, t).start()
+        stats_to(1, t).start()
+
+    other_spaces(send_stats)
     stats_to(1, here).start()
     stats_recv[core, here] = stats_send[...]
     stats_from(1, here).wait_recv()
-    others(spaces, here, lambda t: stats_from(0, t).wait_recv())
-    others(spaces, here, lambda t: stats_from(1, t).wait_recv())
+    other_spaces(lambda t: stats_from(0, t).wait_recv())
+    other_spaces(lambda t: stats_from(1, t).wait_recv())
     packed = stats_recv[0, 0] + stats_recv[1, 0]
     for t in range(1, spaces):
         packed = packed + (stats_recv[0, t] + stats_recv[1, t])
     stats = jnp.concatenate(
         [packed[:, members * g : members * (g + 1)] for g in range(members // 8)], axis=0
     )
-
-    def times(a, b):
-        return jnp.dot(a, b, precision=HIGHEST, preferred_element_type=F32)
 
     row_id = lax.broadcasted_iota(jnp.int32, (members, members), 0)
     col_id = lax.broadcasted_iota(jnp.int32, (members, members), 1)
@@ -391,11 +498,13 @@
     system = identity + covar / (members - 1.0)
     magnitude = jnp.sqrt(jnp.sum(system * system, axis=(0, 1), keepdims=True))
     iterate = system / magnitude
-    inverse_root = identity
-    for _ in range(NS_STEPS):
+
+    def newton(_, pair_of):
+        iterate, inverse_root = pair_of
         factor = 1.5 * identity - 0.5 * times(inverse_root, iterate)
-        iterate = times(iterate, factor)
-        inverse_root = times(factor, inverse_root)
+        return times(iterate, factor), times(factor, inverse_root)
+
+    _, inverse_root = lax.fori_loop(0, NS_STEPS, newton, (iterate, identity))
     root_part = inverse_root / jnp.sqrt(magnitude)
     inverse_full = times(inverse_root, inverse_root) / magnitude
     shift = times(inverse_full, stats)[:, members - 1 : members] / (members - 1.0)
@@ -403,19 +512,27 @@
     mixing = combined - jnp.mean(combined, axis=0, keepdims=True) + 1.0 / members
     mixing_ref[...] = mixing
 
-    others(members, me, lambda i: there_from(i).wait_recv())
+    other_members(lambda i: there_from(i).wait_recv())
     count = FIELDS * 8
-    block = jnp.concatenate(
-        [pointwise.reshape(members * count, LANES)[pl.ds(k, members, stride=count), :] for k in range(count)],
-        axis=1,
-    )
-    analysed = lax.dot_general(
-        mixing, block, (((0,), (0,)), ((), ())), precision=HIGHEST, preferred_element_type=F32
-    )
-    for k in range(count):
-        mixed.reshape(members * count, LANES)[pl.ds(k, members, stride=count), :] = (
-            analysed[:, k * LANES : (k + 1) * LANES]
-        )
+    sources, targets = (ref.reshape(members * count, LANES) for ref in (pointwise, mixed))
+    mix0, mix1 = split(mixing, 2)
+    weights = jnp.concatenate([mix0, mix1, mix0, mix1], axis=0)
+
+    def mix_field(f, carry):
+        def lines(k):
+            return pl.ds(8 * f + k, members, stride=count)
+
+        block = jnp.concatenate([sources[lines(k), :] for k in range(8)], axis=1)
+        block0, block1 = split(block, 2)
+        analysed = lax.dot_general(
+            weights, jnp.concatenate([block0, block0, block1, block1], axis=0),
+            (((0,), (0,)), ((), ())), preferred_element_type=F32,
+        )
+        for k in range(8):
+            targets[lines(k), :] = analysed[:, k * LANES : (k + 1) * LANES]
+        return carry
+
+    lax.fori_loop(0, FIELDS, mix_field, 0)
 
     def back(j):
         return pltpu.make_async_remote_copy(
@@ -431,7 +548,7 @@
             device_id=(p, here), device_id_type=MESH,
         )
 
-    others(members, me, lambda j: back(j).start())
+    other_members(lambda j: back(j).start())
     returned[me] = mixed[me]
 
     def finish_send(n, carry):
@@ -441,19 +558,19 @@
         return carry
 
     lax.fori_loop(0, BATCHES, finish_send, 0)
-    others(members, me, lambda p: there(p).wait_send())
+    other_members(lambda p: there(p).wait_send())
     beam_to(1, here).wait_send()
     stats_to(1, here).wait_send()
     for half in range(2):
-        others(spaces, here, lambda t: beam_to(half, t).wait_send())
-        others(spaces, here, lambda t: stats_to(half, t).wait_send())
-    others(members, me, lambda p: share_to(p).wait_send())
-    others(members, me, lambda p: back_from(p).wait_recv())
+        other_spaces(lambda t: beam_to(half, t).wait_send())
+        other_spaces(lambda t: stats_to(half, t).wait_send())
+    other_members(lambda p: share_to(p).wait_send())
+    other_members(lambda p: back_from(p).wait_recv())
     for p in range(members):
         r, q = divmod(p, members // 2)
         for f in range(FIELDS):
             out_ref[f, pl.ds(16 * q + r, 8, stride=2), :] = returned[p, f]
-    others(members, me, lambda j: back(j).wait_send())
+    other_members(lambda j: back(j).wait_send())
 
 
 def shards(members, spaces, realization_fields, viscosity, cell_index, beam_id, los_weight, observed, obs_variance):
@@ -488,9 +605,9 @@
             pltpu.VMEM((9, LINES + BATCH, LANES), F32),
             pltpu.VMEM(block, F32),
             pltpu.VMEM(block, F32),
-            pltpu.VMEM((2, BATCHES, 32, LANES), F32),
+            pltpu.VMEM((2, BATCHES + 1, 32, LANES), F32),
             pltpu.VMEM((BATCHES, 32, LANES), F32),
-            pltpu.VMEM((2 * BATCHES, 16 * LANES, BEAM_COLS), BF16),
+            pltpu.VMEM((4 * BATCHES, 8 * LANES, BEAM_COLS), BF16),
             pltpu.VMEM((2 * PARTS * BEAM_ROWS, BEAM_COLS), F32),
             pltpu.VMEM((2, spaces) + share, F32),
             pltpu.VMEM((2, spaces) + share, F32),
@@ -500,7 +617,7 @@
             pltpu.VMEM((2, spaces, 8, LANES), F32),
             pltpu.VMEM(block, F32),
             pltpu.VMEM(block, F32),
-            dma(7),
+            dma(7), pltpu.SemaphoreType.REGULAR((RELAYS,)),
             dma(2, BATCHES), dma(2, BATCHES),
             dma(BATCHES), dma(BATCHES),
             dma(members), dma(members),

time: 69.2 us -> 65.8 us (0.951)
  Pallas kernels: 65.9 us -> 62.5 us
    pallas_call x1, Pallas kernels: 65.9 us -> 62.5 us  [shards(): pl.pallas_call(functools.partial(kernel, members, spaces), out_shape=(jax...]
where the time goes in v4:
time: 65.8 us; the launch traced here: 65.6 us
  Pallas kernels  62.5 us (95%)
  local copies, waits for them, and re-layouts  2.48 us (4%)
    pallas_call x1, Pallas kernels, shards(): pl.pallas_call(functools.partial(kernel, members, spaces), out_shape=(jax...  62.5 us
    unnamed x4, local copies, waits for them, and re-layouts  2.48 us

profile of v4, /device:TPU:1, one launch (start us, length us, event | category | flops | bytes accessed | tf_op | source)
XLA Modules:
  0.0 65.6 jit_solution(11776015567719966449)
XLA Ops:
  0.6 62.5 %shard_map.86 = (f32[4,256,128]{2,1,0:T(8,128)}, f32[32,32]{1,0:T(8,128)}) custom-call(f32[4,256,128]{2,1,0:T(8,128)} %bitcast.22, f32[256,128]{1,0:T(8,128)} %bitcast.25, s32[512,128]{1,0:T(8,128)} %bitcast.23, s32[512,128]{1,0:T(8,128)} %bitcast.24, f32[3,512,128]{2,1,0:T(8,128)} %bitcast.20, f32[128,128]{1,0:T(8,128)} %bitcast.26, f32[128,128]{1,0:T(8,128)} %bitcast.27), custom_call_target="tpu_custom_call" | custom-call | tf_op jit(solution)/shard_map/pallas_call | solution.py:587
  63.1 0.0 copy-start
  63.2 1.9 %copy.14 = f32[1,4,2,16384]{3,2,1,0:T(2,128)} copy(f32[1,4,2,16384]{3,2,1,0:T(2,128)} %bitcast.21) | data formatting | bytes 1048576
  65.0 0.0 copy-done
  65.0 0.6 copy.15
Async XLA Ops:
  63.1 1.9 %copy-start = (f32[32,32]{1,0:T(8,128)S(1)}, f32[32,32]{1,0:T(8,128)}, u32[]{:S(2)}) copy-start(f32[32,32]{1,0:T(8,128)} %get-tuple-element.9) | copy-start | bytes 12292

commit v5 on v4

--- a/solution.py
+++ b/solution.py
@@ -102,14 +102,14 @@
     def ring(i):
         return lax.rem(6 - i + jnp.where(i >= 2, 7 - 2 * i, 0), SIDE)
 
-    def other_members(act):
+    def other_members(act, first=0, last=members - 1):
         def one(i, carry):
             flip = 1 - lax.rem(i, 2)
             side = core + flip - 2 * core * flip
             act(device_at(across + ring(i // 8), along + ring(lax.rem(i // 2, SIDE)), side))
             return carry
 
-        lax.fori_loop(0, members - 1, one, 0)
+        lax.fori_loop(first, last, one, 0)
 
     def other_spaces(act):
         def one(j, carry):
@@ -118,6 +118,10 @@
             return carry
 
         lax.fori_loop(0, spaces - 1, one, 0)
+
+    def finish(buffer, count, semaphore):
+        part = buffer.at[pl.ds(0, count)]
+        pltpu.make_async_copy(part, part, semaphore).wait()
 
     barrier = pltpu.get_barrier_semaphore()
 
@@ -287,15 +291,8 @@
     def there(p):
         return pltpu.make_async_remote_copy(
             src_ref=forecast.at[p], dst_ref=pointwise.at[me],
-            send_sem=there_send_sem.at[p], recv_sem=there_recv_sem.at[me],
+            send_sem=there_send_sem, recv_sem=there_recv_sem,
             device_id=(p, here), device_id_type=MESH,
-        )
-
-    def there_from(i):
-        return pltpu.make_async_remote_copy(
-            src_ref=forecast.at[i], dst_ref=pointwise.at[i],
-            send_sem=there_send_sem.at[i], recv_sem=there_recv_sem.at[i],
-            device_id=(i, here), device_id_type=MESH,
         )
 
     scatter[...] = jnp.zeros_like(scatter)
@@ -352,22 +349,6 @@
         def _():
             hand_on(RELAYS)
 
-        def send_row(r, inner):
-            def send_block(h, inner):
-                block = members // 2 * r + 4 * (n - BATCHES // 2) + h
-
-                @pl.when(block != me)
-                def _():
-                    there(block).start()
-
-                return inner
-
-            return lax.fori_loop(0, 4, send_block, inner)
-
-        @pl.when(jnp.logical_and(n >= BATCHES // 2, n < BATCHES))
-        def _():
-            lax.fori_loop(0, 2, send_row, 0)
-
         return carry
 
     lax.fori_loop(0, LAG, first_batch, 0)
@@ -375,19 +356,12 @@
     for half in range(2):
         first = 2 * BEAM_ROWS * half
         total = scatter[first : first + BEAM_ROWS] + scatter[first + BEAM_ROWS : first + 2 * BEAM_ROWS]
-        beam_send[half] = total.reshape(beam_send.shape[1:])
+        beam_send[pl.ds(spaces * half, spaces)] = total.reshape((spaces,) + beam_send.shape[1:])
 
     def beam_to(half, t):
         return pltpu.make_async_remote_copy(
-            src_ref=beam_send.at[half, t], dst_ref=beam_recv.at[half, here],
-            send_sem=beam_send_sem.at[half, t], recv_sem=beam_recv_sem.at[half, here],
-            device_id=(pair if half else me, t), device_id_type=MESH,
-        )
-
-    def beam_from(half, t):
-        return pltpu.make_async_remote_copy(
-            src_ref=beam_send.at[half, t], dst_ref=beam_recv.at[half, t],
-            send_sem=beam_send_sem.at[half, t], recv_sem=beam_recv_sem.at[half, t],
+            src_ref=beam_send.at[spaces * half + t], dst_ref=beam_recv.at[spaces * half + here],
+            send_sem=beam_send_sem, recv_sem=beam_recv_sem,
             device_id=(pair if half else me, t), device_id_type=MESH,
         )
 
@@ -397,14 +371,13 @@
 
     other_spaces(send_share)
     beam_to(1, here).start()
-    beam_recv[0, here] = beam_send[0, here]
+    beam_recv[here] = beam_send[here]
+    other_members(lambda p: there(p).start(), 0, members // 2)
     pointwise[me] = forecast[me]
-    beam_from(1, here).wait_recv()
-    other_spaces(lambda t: beam_from(0, t).wait_recv())
-    other_spaces(lambda t: beam_from(1, t).wait_recv())
-    predicted = beam_recv[0, 0] + beam_recv[1, 0]
+    finish(beam_recv, 2 * spaces - 1, beam_recv_sem)
+    predicted = beam_recv[0] + beam_recv[spaces]
     for t in range(1, spaces):
-        predicted = predicted + (beam_recv[0, t] + beam_recv[1, t])
+        predicted = predicted + (beam_recv[t] + beam_recv[spaces + t])
 
     for half in range(2):
         share[half] = predicted[:, half * LANES : (half + 1) * LANES]
@@ -415,20 +388,13 @@
     def share_to(p):
         return pltpu.make_async_remote_copy(
             src_ref=share.at[lax.rem(p, 2)], dst_ref=slot(me),
-            send_sem=gather_send_sem.at[p], recv_sem=gather_recv_sem.at[me],
+            send_sem=gather_send_sem, recv_sem=gather_recv_sem,
             device_id=(p, here), device_id_type=MESH,
-        )
-
-    def share_from(i):
-        return pltpu.make_async_remote_copy(
-            src_ref=share.at[core], dst_ref=slot(i),
-            send_sem=gather_send_sem.at[i], recv_sem=gather_recv_sem.at[i],
-            device_id=(i, here), device_id_type=MESH,
         )
 
     other_members(lambda p: share_to(p).start())
     gathered[pl.ds(pl.multiple_of(8 * me, 8), 8), :] = share[core]
-    other_members(lambda i: share_from(i).wait_recv())
+    finish(gathered, 8 * (members - 1), gather_recv_sem)
 
     every = jnp.concatenate(
         [gathered[pl.ds(sub, members, stride=8), :] for sub in range(8)], axis=1
@@ -459,18 +425,12 @@
     partial = term(0, 0) + ((term(0, 1) + term(1, 0)) + (term(1, 1) + (term(0, 2) + term(2, 0))))
     stats_send[...] = jnp.concatenate([partial[8 * g : 8 * g + 8] for g in range(members // 8)], axis=1)
 
-    def stats_copy(other, t, origin_core, origin):
+    def stats_to(other, t):
         return pltpu.make_async_remote_copy(
-            src_ref=stats_send, dst_ref=stats_recv.at[origin_core, origin],
-            send_sem=stats_send_sem.at[other, t], recv_sem=stats_recv_sem.at[origin_core, origin],
+            src_ref=stats_send, dst_ref=stats_recv.at[spaces * core + here],
+            send_sem=stats_send_sem, recv_sem=stats_recv_sem,
             device_id=(pair if other else me, t), device_id_type=MESH,
         )
-
-    def stats_to(other, t):
-        return stats_copy(other, t, core, here)
-
-    def stats_from(other, t):
-        return stats_copy(other, t, 1 - core if other else core, t)
 
     def send_stats(t):
         stats_to(0, t).start()
@@ -478,13 +438,12 @@
 
     other_spaces(send_stats)
     stats_to(1, here).start()
-    stats_recv[core, here] = stats_send[...]
-    stats_from(1, here).wait_recv()
-    other_spaces(lambda t: stats_from(0, t).wait_recv())
-    other_spaces(lambda t: stats_from(1, t).wait_recv())
-    packed = stats_recv[0, 0] + stats_recv[1, 0]
+    other_members(lambda p: there(p).start(), members // 2)
+    stats_recv[spaces * core + here] = stats_send[...]
+    finish(stats_recv, 2 * spaces - 1, stats_recv_sem)
+    packed = stats_recv[0] + stats_recv[spaces]
     for t in range(1, spaces):
-        packed = packed + (stats_recv[0, t] + stats_recv[1, t])
+        packed = packed + (stats_recv[t] + stats_recv[spaces + t])
     stats = jnp.concatenate(
         [packed[:, members * g : members * (g + 1)] for g in range(members // 8)], axis=0
     )
@@ -512,7 +471,7 @@
     mixing = combined - jnp.mean(combined, axis=0, keepdims=True) + 1.0 / members
     mixing_ref[...] = mixing
 
-    other_members(lambda i: there_from(i).wait_recv())
+    finish(pointwise, members - 1, there_recv_sem)
     count = FIELDS * 8
     sources, targets = (ref.reshape(members * count, LANES) for ref in (pointwise, mixed))
     mix0, mix1 = split(mixing, 2)
@@ -537,15 +496,8 @@
     def back(j):
         return pltpu.make_async_remote_copy(
             src_ref=mixed.at[j], dst_ref=returned.at[me],
-            send_sem=back_send_sem.at[j], recv_sem=back_recv_sem.at[me],
+            send_sem=back_send_sem, recv_sem=back_recv_sem,
             device_id=(j, here), device_id_type=MESH,
-        )
-
-    def back_from(p):
-        return pltpu.make_async_remote_copy(
-            src_ref=mixed.at[p], dst_ref=returned.at[p],
-            send_sem=back_send_sem.at[p], recv_sem=back_recv_sem.at[p],
-            device_id=(p, here), device_id_type=MESH,
         )
 
     other_members(lambda j: back(j).start())
@@ -558,19 +510,16 @@
         return carry
 
     lax.fori_loop(0, BATCHES, finish_send, 0)
-    other_members(lambda p: there(p).wait_send())
-    beam_to(1, here).wait_send()
-    stats_to(1, here).wait_send()
-    for half in range(2):
-        other_spaces(lambda t: beam_to(half, t).wait_send())
-        other_spaces(lambda t: stats_to(half, t).wait_send())
-    other_members(lambda p: share_to(p).wait_send())
-    other_members(lambda p: back_from(p).wait_recv())
+    finish(forecast, members - 1, there_send_sem)
+    finish(beam_send, 2 * spaces - 1, beam_send_sem)
+    finish(stats_recv, 2 * spaces - 1, stats_send_sem)
+    finish(gathered, 8 * (members - 1), gather_send_sem)
+    finish(returned, members - 1, back_recv_sem)
     for p in range(members):
         r, q = divmod(p, members // 2)
         for f in range(FIELDS):
             out_ref[f, pl.ds(16 * q + r, 8, stride=2), :] = returned[p, f]
-    other_members(lambda j: back(j).wait_send())
+    finish(mixed, members - 1, back_send_sem)
 
 
 def shards(members, spaces, realization_fields, viscosity, cell_index, beam_id, los_weight, observed, obs_variance):
@@ -609,22 +558,18 @@
             pltpu.VMEM((BATCHES, 32, LANES), F32),
             pltpu.VMEM((4 * BATCHES, 8 * LANES, BEAM_COLS), BF16),
             pltpu.VMEM((2 * PARTS * BEAM_ROWS, BEAM_COLS), F32),
-            pltpu.VMEM((2, spaces) + share, F32),
-            pltpu.VMEM((2, spaces) + share, F32),
+            pltpu.VMEM((2 * spaces,) + share, F32),
+            pltpu.VMEM((2 * spaces,) + share, F32),
             pltpu.VMEM((2, share[0], LANES), F32),
             pltpu.VMEM((members * share[0], LANES), F32),
             pltpu.VMEM((8, LANES), F32),
-            pltpu.VMEM((2, spaces, 8, LANES), F32),
+            pltpu.VMEM((2 * spaces, 8, LANES), F32),
             pltpu.VMEM(block, F32),
             pltpu.VMEM(block, F32),
             dma(7), pltpu.SemaphoreType.REGULAR((RELAYS,)),
             dma(2, BATCHES), dma(2, BATCHES),
             dma(BATCHES), dma(BATCHES),
-            dma(members), dma(members),
-            dma(2, spaces), dma(2, spaces),
-            dma(members), dma(members),
-            dma(2, spaces), dma(2, spaces),
-            dma(members), dma(members),
+            *([pltpu.SemaphoreType.DMA] * 10),
         ],
         compiler_params=pltpu.CompilerParams(
             collective_id=0, has_side_effects=True, vmem_limit_bytes=60 << 20

time: 65.8 us -> 61.8 us (0.939)
  Pallas kernels: 62.5 us -> 58.5 us
    pallas_call x1, Pallas kernels: 62.5 us -> 58.5 us  [shards(): pl.pallas_call(functools.partial(kernel, members, spaces), out_shape=(jax...]
where the time goes in v5:
time: 61.8 us; the launch traced here: 61.6 us
  Pallas kernels  58.5 us (95%)
  local copies, waits for them, and re-layouts  2.48 us (4%)
  between operations  0.65 us (1%)
    pallas_call x1, Pallas kernels, shards(): pl.pallas_call(functools.partial(kernel, members, spaces), out_shape=(jax...  58.5 us
    unnamed x4, local copies, waits for them, and re-layouts  2.48 us

profile of v5, /device:TPU:1, one launch (start us, length us, event | category | flops | bytes accessed | tf_op | source)
XLA Modules:
  0.0 61.6 jit_solution(16226999363229214059)
XLA Ops:
  0.6 58.5 %shard_map.86 = (f32[4,256,128]{2,1,0:T(8,128)}, f32[32,32]{1,0:T(8,128)}) custom-call(f32[4,256,128]{2,1,0:T(8,128)} %bitcast.22, f32[256,128]{1,0:T(8,128)} %bitcast.25, s32[512,128]{1,0:T(8,128)} %bitcast.23, s32[512,128]{1,0:T(8,128)} %bitcast.24, f32[3,512,128]{2,1,0:T(8,128)} %bitcast.20, f32[128,128]{1,0:T(8,128)} %bitcast.26, f32[128,128]{1,0:T(8,128)} %bitcast.27), custom_call_target="tpu_custom_call" | custom-call | tf_op jit(solution)/shard_map/pallas_call | solution.py:536
  59.1 0.0 copy-start
  59.2 1.9 %copy.14 = f32[1,4,2,16384]{3,2,1,0:T(2,128)} copy(f32[1,4,2,16384]{3,2,1,0:T(2,128)} %bitcast.21) | data formatting | bytes 1048576
  61.0 0.0 copy-done
  61.0 0.6 copy.15
Async XLA Ops:
  59.1 1.9 %copy-start = (f32[32,32]{1,0:T(8,128)S(1)}, f32[32,32]{1,0:T(8,128)}, u32[]{:S(2)}) copy-start(f32[32,32]{1,0:T(8,128)} %get-tuple-element.9) | copy-start | bytes 12292

commit v6 on v5

--- a/solution.py
+++ b/solution.py
@@ -99,25 +99,22 @@
     def device_at(x, y, side):
         return 2 * (SIDE * lax.rem(x, SIDE) + lax.rem(y, SIDE)) + side
 
-    def ring(i):
-        return lax.rem(6 - i + jnp.where(i >= 2, 7 - 2 * i, 0), SIDE)
+    steps_x = [lax.rem(across + i, SIDE) * (2 * SIDE) for i in range(SIDE)]
+    steps_y = [lax.rem(along + i, SIDE) * 2 for i in range(SIDE)]
+    sides = [core, 1 - core]
+    far_first = sorted(
+        ((x, y, side) for x in range(SIDE) for y in range(SIDE) for side in range(2)),
+        key=lambda step: -min(step[0], SIDE - step[0]) - min(step[1], SIDE - step[1]),
+    )
+    far_first.remove((0, 0, 0))
 
     def other_members(act, first=0, last=members - 1):
-        def one(i, carry):
-            flip = 1 - lax.rem(i, 2)
-            side = core + flip - 2 * core * flip
-            act(device_at(across + ring(i // 8), along + ring(lax.rem(i // 2, SIDE)), side))
-            return carry
-
-        lax.fori_loop(first, last, one, 0)
+        for x, y, side in far_first[first:last]:
+            act(steps_x[x] + steps_y[y] + sides[side])
 
     def other_spaces(act):
-        def one(j, carry):
-            step = (j + 1) // 2
-            act(lax.rem(here + spaces // 2 + jnp.where(lax.rem(j, 2) == 1, spaces - step, step), spaces))
-            return carry
-
-        lax.fori_loop(0, spaces - 1, one, 0)
+        for step in sorted(range(1, spaces), key=lambda step: -min(step, spaces - step)):
+            act(lax.rem(here + step, spaces))
 
     def finish(buffer, count, semaphore):
         part = buffer.at[pl.ds(0, count)]
@@ -463,7 +460,8 @@
         factor = 1.5 * identity - 0.5 * times(inverse_root, iterate)
         return times(iterate, factor), times(factor, inverse_root)
 
-    _, inverse_root = lax.fori_loop(0, NS_STEPS, newton, (iterate, identity))
+    factor = 1.5 * identity - 0.5 * iterate
+    _, inverse_root = lax.fori_loop(1, NS_STEPS, newton, (times(iterate, factor), factor))
     root_part = inverse_root / jnp.sqrt(magnitude)
     inverse_full = times(inverse_root, inverse_root) / magnitude
     shift = times(inverse_full, stats)[:, members - 1 : members] / (members - 1.0)

time: 61.8 us -> 60.3 us (0.976)
  Pallas kernels: 58.5 us -> 57.1 us
    pallas_call x1, Pallas kernels: 58.5 us -> 57.1 us  [shards(): pl.pallas_call(functools.partial(kernel, members, spaces), out_shape=(jax...]
where the time goes in v6:
time: 60.3 us; the launch traced here: 60.2 us
  Pallas kernels  57.1 us (95%)
  local copies, waits for them, and re-layouts  2.48 us (4%)
  between operations  0.65 us (1%)
    pallas_call x1, Pallas kernels, shards(): pl.pallas_call(functools.partial(kernel, members, spaces), out_shape=(jax...  57.1 us
    unnamed x4, local copies, waits for them, and re-layouts  2.48 us

profile of v6, /device:TPU:1, one launch (start us, length us, event | category | flops | bytes accessed | tf_op | source)
XLA Modules:
  0.0 60.2 jit_solution(5127676455624276216)
XLA Ops:
  0.6 57.1 %shard_map.86 = (f32[4,256,128]{2,1,0:T(8,128)}, f32[32,32]{1,0:T(8,128)}) custom-call(f32[4,256,128]{2,1,0:T(8,128)} %bitcast.22, f32[256,128]{1,0:T(8,128)} %bitcast.25, s32[512,128]{1,0:T(8,128)} %bitcast.23, s32[512,128]{1,0:T(8,128)} %bitcast.24, f32[3,512,128]{2,1,0:T(8,128)} %bitcast.20, f32[128,128]{1,0:T(8,128)} %bitcast.26, f32[128,128]{1,0:T(8,128)} %bitcast.27), custom_call_target="tpu_custom_call" | custom-call | tf_op jit(solution)/shard_map/pallas_call | solution.py:534
  57.7 0.0 copy-start
  57.7 1.9 %copy.14 = f32[1,4,2,16384]{3,2,1,0:T(2,128)} copy(f32[1,4,2,16384]{3,2,1,0:T(2,128)} %bitcast.21) | data formatting | bytes 1048576
  59.6 0.0 copy-done
  59.6 0.6 %copy.15 = f32[32,32]{1,0:T(8,128)} copy(f32[32,32]{1,0:T(8,128)S(1)} %copy-done) | data formatting | bytes 8192
Async XLA Ops:
  57.7 1.9 %copy-start = (f32[32,32]{1,0:T(8,128)S(1)}, f32[32,32]{1,0:T(8,128)}, u32[]{:S(2)}) copy-start(f32[32,32]{1,0:T(8,128)} %get-tuple-element.9) | copy-start | bytes 12292

commit v7 on v6

--- a/solution.py
+++ b/solution.py
@@ -68,11 +68,11 @@
 def kernel(
     members, spaces,
     fields_hbm, visc_hbm, cell_hbm, beam_hbm, weight_hbm, observed_hbm, variance_hbm,
-    out_ref, mixing_ref,
-    fields_ref, visc_ref, cell_ref, beam_ref, weight_ref, observed_ref, variance_ref,
+    out_hbm, mixing_ref,
+    out_ref, fields_ref, visc_ref, cell_ref, beam_ref, weight_ref, observed_ref, variance_ref,
     own, low, high, forecast, pointwise, sight, pair_sight, columns, scatter,
     beam_send, beam_recv, share, gathered, stats_send, stats_recv, mixed, returned,
-    load_sem, relay_sem, halo_send_sem, halo_recv_sem, sight_send_sem, sight_recv_sem,
+    load_sem, store_sem, relay_sem, halo_send_sem, halo_recv_sem, sight_send_sem, sight_recv_sem,
     there_send_sem, there_recv_sem, beam_send_sem, beam_recv_sem,
     gather_send_sem, gather_recv_sem, stats_send_sem, stats_recv_sem, back_send_sem, back_recv_sem,
 ):
@@ -513,10 +513,16 @@
     finish(stats_recv, 2 * spaces - 1, stats_send_sem)
     finish(gathered, 8 * (members - 1), gather_send_sem)
     finish(returned, members - 1, back_recv_sem)
-    for p in range(members):
-        r, q = divmod(p, members // 2)
-        for f in range(FIELDS):
+    stores = [
+        pltpu.make_async_copy(out_ref.at[f], out_hbm.at[f], store_sem.at[f]) for f in range(FIELDS)
+    ]
+    for f in range(FIELDS):
+        for p in range(members):
+            r, q = divmod(p, members // 2)
             out_ref[f, pl.ds(16 * q + r, 8, stride=2), :] = returned[p, f]
+        stores[f].start()
+    for store in stores:
+        store.wait()
     finish(mixed, members - 1, back_send_sem)
 
 
@@ -538,8 +544,9 @@
             jax.ShapeDtypeStruct((members, members), F32),
         ),
         in_specs=[pl.BlockSpec(memory_space=pl.ANY)] * 7,
-        out_specs=(vmem, vmem),
+        out_specs=(pl.BlockSpec(memory_space=pl.ANY), vmem),
         scratch_shapes=[
+            pltpu.VMEM((fields, rows * lines, LANES), F32),
             pltpu.VMEM((fields, rows * lines, LANES), F32),
             pltpu.VMEM((rows * lines, LANES), F32),
             pltpu.VMEM((samples, LANES), jnp.int32),
@@ -564,7 +571,7 @@
             pltpu.VMEM((2 * spaces, 8, LANES), F32),
             pltpu.VMEM(block, F32),
             pltpu.VMEM(block, F32),
-            dma(7), pltpu.SemaphoreType.REGULAR((RELAYS,)),
+            dma(7), dma(fields), pltpu.SemaphoreType.REGULAR((RELAYS,)),
             dma(2, BATCHES), dma(2, BATCHES),
             dma(BATCHES), dma(BATCHES),
             *([pltpu.SemaphoreType.DMA] * 10),

time: 60.3 us -> 60.9 us (level)
  no operation moved by 1% of the time
where the time goes in v7:
time: 60.9 us; the launch traced here: 60.8 us
  Pallas kernels  57.7 us (95%)
  local copies, waits for them, and re-layouts  2.48 us (4%)
  between operations  0.65 us (1%)
    pallas_call x1, Pallas kernels, shards(): pl.pallas_call(functools.partial(kernel, members, spaces), out_shape=(jax...  57.7 us
    unnamed x4, local copies, waits for them, and re-layouts  2.48 us

profile of v7, /device:TPU:1, one launch (start us, length us, event | category | flops | bytes accessed | tf_op | source)
XLA Modules:
  0.0 60.8 jit_solution(6223606959964049525)
XLA Ops:
  0.6 57.7 %shard_map.86 = (f32[4,256,128]{2,1,0:T(8,128)}, f32[32,32]{1,0:T(8,128)}) custom-call(f32[4,256,128]{2,1,0:T(8,128)} %bitcast.22, f32[256,128]{1,0:T(8,128)} %bitcast.25, s32[512,128]{1,0:T(8,128)} %bitcast.23, s32[512,128]{1,0:T(8,128)} %bitcast.24, f32[3,512,128]{2,1,0:T(8,128)} %bitcast.20, f32[128,128]{1,0:T(8,128)} %bitcast.26, f32[128,128]{1,0:T(8,128)} %bitcast.27), custom_call_target="tpu_custom_call" | custom-call | tf_op jit(solution)/shard_map/pallas_call | solution.py:540
  58.3 0.0 copy-start
  58.3 1.9 %copy.14 = f32[1,4,2,16384]{3,2,1,0:T(2,128)} copy(f32[1,4,2,16384]{3,2,1,0:T(2,128)} %bitcast.21) | data formatting | bytes 1048576
  60.2 0.0 copy-done
  60.2 0.6 copy.15
Async XLA Ops:
  58.3 1.9 %copy-start = (f32[32,32]{1,0:T(8,128)S(1)}, f32[32,32]{1,0:T(8,128)}, u32[]{:S(2)}) copy-start(f32[32,32]{1,0:T(8,128)} %get-tuple-element.9) | copy-start | bytes 12292
